TPU v7x, 256 devices: a whole 4x4x8 slice. The times are simulated.
256 devices in a mesh: row: 8 (over y, core), col: 32 (over x, z).
Axes of the slice: x: 4, y: 4, z: 8, core: 2. Of those that a mesh axis runs over, the one named last changes fastest.
Arguments:
- amplitudes: float32 [8192, 4096], P('row', 'col'), may hold values from -6 to 6
- integrals: float32 [4096, 16384], P(None, 'col'), may hold values from -0.125 to 0.125
- screen: int32 [32, 128], P(None, 'col'), may hold values 0 or 1
- slab_order: int32 [32], replicated, may hold values from 0 to 31, each once
- weights: float32 [8192, 16384], P('row', 'col'), may hold values from 0.05 to 1
Outputs:
- ladder: float32 [8192, 16384], P('row', 'col')
- energy: float32 [], replicated
Inputs may be any that keep to these rules, and one draw needn't show every extreme that they name: `slab_order`: each of 0 to 31 appears once.
All inputs are finite; a program needn't handle non-finite values. No bound on the sum of `screen` on one device may be relied on, other than what follows from the above.
Results may differ from a plain program's by a relative error of at most 0.00007.
Values sent between devices are 32-bit elements; how exact they have to be, the bound alone decides.
No kernel may reach another device: no remote copies, remote signals or barrier semaphores. Data moves between devices by JAX's collectives and lax.ppermute only.
A program may use at most 128 MiB of HBM per device.

v0:
```python
import jax
import jax.numpy as jnp
from jax import lax
from jax.sharding import PartitionSpec as P


def local(amplitudes, integrals, screen, slab_order, weights):
    ktiles = screen.shape[0]
    ncols = screen.shape[1]
    tile_width = integrals.shape[0] // ktiles
    factor = screen.astype(jnp.float32)[:, None, :, None]
    masked = (integrals.reshape(ktiles, tile_width, ncols, tile_width) * factor).reshape(
        ktiles, tile_width, ncols * tile_width
    )
    placed = jnp.take(masked, slab_order, axis=0).reshape(ktiles * tile_width, ncols * tile_width)
    total = jnp.dot(
        lax.all_gather(amplitudes, "col", axis=1, tiled=True),
        placed,
        precision=lax.Precision.HIGHEST,
        preferred_element_type=jnp.float32,
    )
    ladder = 0.5 * total
    all_cells = amplitudes.shape[0] * lax.axis_size("row") * placed.shape[1] * lax.axis_size("col")
    energy = lax.psum(jnp.sum(weights * ladder * ladder), ("row", "col")) / all_cells
    return (ladder, energy)


def solution(mesh):
    return jax.shard_map(
        local,
        mesh=mesh,
        in_specs=(P("row", "col"), P(None, "col"), P(None, "col"), P(), P("row", "col")),
        out_specs=(P("row", "col"), P()),
        check_vma=False,
    )
```

profile of v0, /device:TPU:1, one launch (start us, length us, event | category | flops | bytes accessed | tf_op | source)
XLA Modules:
  0.0 309.5 jit_solution(12734051913290187608)
XLA Ops:
  7.2 0.0 all-gather.2.cloned.1.call-start
  7.2 0.7 all-gather.2.cloned.1.call-update
  7.9 0.7 convert_element_type.3
  8.6 0.1 copy.7
  8.7 0.1 mul.28
  8.8 1.9 copy.8
  10.7 0.7 compare_select_fusion
  11.4 8.3 %broadcast_multiply_fusion = f32[32,128,512]{2,1,0:T(8,128)} fusion(f32[32,128,512]{2,1,0:T(8,128)} %bitcast.13, f32[32,512]{1,0:T(8,128)S(1)} %bitcast.14), kind=kLoop, calls=%fused_computation.2 | loop fusion | flops 2097152 | bytes 16842752 | tf_op jit(solution)/shard_map/mul | solution.py:12
  19.7 0.0 copy-start
  19.7 7.7 %gather_fusion = f32[32,128,512]{2,1,0:T(8,128)} fusion(f32[32,128,512]{2,1,0:T(8,128)} %broadcast_multiply_fusion, s32[1024]{0:T(1024)S(1)} %pad_clamp_fusion), kind=kCustom, calls=%fused_computation | custom fusion | bytes 16777344 | tf_op jit(solution)/shard_map/jit(_take)/gather | solution.py:15
  27.4 0.0 copy-done
  27.4 0.1 broadcast_bitcast_fusion
  27.4 6.0 %bitcast_select_fusion = f32[4096,512]{1,0:T(8,128)} fusion(f32[32,128,512]{2,1,0:T(8,128)} %gather_fusion, pred[4096]{0:T(1024)(128)(4,1)S(1)} %broadcast_bitcast_fusion), kind=kLoop, calls=%fused_computation.1 | loop fusion | flops 2097152 | bytes 16781312 | tf_op jit(solution)/shard_map/jit(_take)/select_n | solution.py:15
  33.4 129.1 %all-gather.2.cloned.1.call-done = f32[1024,4096]{1,0:T(8,128)} async-done(((f32[1024,128]{1,0:T(8,128)}), f32[1024,4096]{1,0:T(8,128)}) %all-gather.2.cloned.1.call-update) | async-done | bytes 16777232 | tf_op jit(solution)/shard_map/all_gather | solution.py:17
  162.5 58.1 %fusion = (f32[]{:T(128)}, f32[1024,512]{0,1:T(8,128)}) fusion(f32[1024,512]{0,1:T(8,128)S(1)} %copy.8, f32[4096,512]{1,0:T(8,128)} %bitcast_select_fusion, f32[1024,4096]{1,0:T(8,128)} %all-gather.2.cloned.1.call-done), kind=kOutput, calls=%fused_computation.4 | convolution fusion | flops 25771900928 | bytes 29360132 | tf_op jit(solution)/shard_map/dot_general | solution.py:16
  220.6 2.9 copy.9
  223.5 77.4 %psum.7 = f32[]{:T(128)} all-reduce(f32[]{:T(128)} %get-tuple-element.4), channel_id=1, replica_groups=mesh['row'=8,'col'=32] {'row','col'}, use_global_device_ids=true, to_apply=%region_1.2 | all-reduce | flops 1 | bytes 8 | tf_op jit(solution)/shard_map/psum | solution.py:24
  (3 shorter events, 0.0 us)
Async XLA Ops:
  7.2 155.3 %all-gather.2.cloned.1.call-start = ((), (), s32[]{:S(2)}) async-start(), calls=%async_computation | async-start | bytes 17301504 | tf_op jit(solution)/shard_map/all_gather | solution.py:17
  19.7 7.7 %copy-start = (s32[32]{0:T(128)S(1)}, s32[32]{0:T(128)}, u32[]{:S(2)}) copy-start(s32[32]{0:T(128)} %param.8) | copy-start | bytes 388
Sparse Core Ops, SparseCore 0:
  10.5 151.9 all-gather.1
where the time goes:
time: 310 us
  waiting for transfers between devices  130 us (42%)
  blocking collectives  77.4 us (25%)
  matrix products  58.1 us (19%)
  between operations  15.8 us (5%)
  other arithmetic  15.6 us (5%)
  local copies, waits for them, and re-layouts  12.8 us (4%)
    all_gather x1, waiting for transfers between devices, local(): lax.all_gather(amplitudes, 'col', axis=1, tiled=True)  129 us
    psum x1, blocking collectives, local(): lax.psum(jnp.sum(weights * ladder * ladder), ('row', 'col')) / all_cells  77.4 us
    dot_general x1, matrix products, local(): jnp.dot(lax.all_gather(amplitudes, 'col', axis=1, tiled=True), placed, pr...  58.1 us
    mul x1, other arithmetic, local(): integrals.reshape(ktiles, tile_width, ncols, tile_width) * factor  8.28 us
    gather x1, local copies, waits for them, and re-layouts, local(): jnp.take(masked, slab_order, axis=0)  7.68 us
    select_n x2, other arithmetic, local(): jnp.take(masked, slab_order, axis=0)  6.63 us
  transfers between devices with their start and end apart: 1, of which 1 were waited for; matrix products, arithmetic and copies ran while one was open for 8% of the time, Pallas kernels for 0%

commit v1 on v0

v1 whole, which is shorter than its diff:
```python
import functools

import jax
import jax.numpy as jnp
from jax import lax
from jax.experimental import pallas as pl
from jax.experimental.pallas import tpu as pltpu
from jax.sharding import PartitionSpec as P

NX, NZ = 4, 8
XPOS = (0, -1, 1, 2)
ZPOS = (0, -1, 1, -2, 2, -3, 3, 4)
T = 128
MIB = 2**20
SLOTS = 16


def shift(v, axis, d):
    pairs = []
    for row in range(lax.axis_size("row")):
        step = d if row % 2 == 0 else -d
        for x in range(NX):
            for z in range(NZ):
                to = (x + step) % NX * NZ + z if axis == "x" else x * NZ + (z + step) % NZ
                pairs.append((row * NX * NZ + x * NZ + z, row * NX * NZ + to))
    return lax.ppermute(v, ("row", "col"), pairs)


def cost(flops):
    return pl.CostEstimate(flops=flops, bytes_accessed=0, transcendentals=0)


def tick_kernel(token_ref, out_ref):
    out_ref[...] = token_ref[...]


class Line:
    def __init__(self, token):
        self.token = token

    def tick(self, flops):
        self.token = pl.pallas_call(
            tick_kernel,
            out_shape=pltpu.VMEM(self.token.shape, self.token.dtype),
            in_specs=whole(1),
            out_specs=whole(1)[0],
            compiler_params=pltpu.CompilerParams(vmem_limit_bytes=MIB),
            cost_estimate=cost(flops),
            name="tick",
        )(*near((self.token,)))

    def hold(self, *values):
        self.token, *values = lax.optimization_barrier((self.token, *values))
        return values[0] if len(values) == 1 else values


def near(values):
    return [pltpu.with_memory_space_constraint(v, pltpu.VMEM) for v in values]


def whole(n):
    return [pl.BlockSpec(memory_space=pltpu.VMEM)] * n


def split(value):
    high = value.astype(jnp.bfloat16)
    return high, (value - high.astype(jnp.float32)).astype(jnp.bfloat16)


def pack_kernel(runs, *refs):
    out_ref, start = refs[-1], 0
    for i, first, end in runs:
        out_ref[pl.ds(start, end - first), :] = refs[i][pl.ds(first, end - first), :]
        start += end - first


def pack(runs):
    arrays = list({id(array): array for array, _, _ in runs}.values())
    places = {id(array): i for i, array in enumerate(arrays)}
    runs = [(places[id(array)], first, end) for array, first, end in runs]
    height = sum(end - first for _, first, end in runs)
    return pl.pallas_call(
        functools.partial(pack_kernel, runs),
        out_shape=pltpu.VMEM((height, T), jnp.float32),
        in_specs=whole(len(arrays)),
        out_specs=whole(1)[0],
        compiler_params=pltpu.CompilerParams(vmem_limit_bytes=MIB),
        cost_estimate=cost(1),
        name="pack",
    )(*near(arrays))


def prepare_kernel(order_ref, screen_ref, b_ref, high_ref, low_ref, slabs, arrived):
    slots, _, width = slabs.shape
    count = b_ref.shape[0] // T

    def copy(i):
        source = b_ref.at[pl.ds(pl.multiple_of(order_ref[i] * T, T), T), :]
        return pltpu.make_async_copy(source, slabs.at[i % slots], arrived.at[i % slots])

    @pl.loop(0, slots)
    def _(i):
        copy(i).start()

    @pl.loop(0, count)
    def _(i):
        copy(i).wait()
        rows = pl.ds(pl.multiple_of(i * T, T), T)
        for n in range(width // T):
            columns = pl.ds(n * T, T)
            kept = slabs[i % slots, :, columns] * screen_ref[order_ref[i], n].astype(jnp.float32)
            high_ref[rows, columns], low_ref[rows, columns] = split(kept)

        @pl.when(i + slots < count)
        def _():
            copy(i + slots).start()


def prepare(order, screen, integrals):
    depth, width = integrals.shape
    return pl.pallas_call(
        prepare_kernel,
        out_shape=[pltpu.VMEM((depth, width), jnp.bfloat16)] * 2,
        in_specs=[pl.BlockSpec(memory_space=pltpu.SMEM)] * 2 + [pl.BlockSpec(memory_space=pltpu.HBM)],
        out_specs=whole(2),
        scratch_shapes=[pltpu.VMEM((SLOTS, T, width), jnp.float32), pltpu.SemaphoreType.DMA((SLOTS,))],
        cost_estimate=cost(1),
        compiler_params=pltpu.CompilerParams(vmem_limit_bytes=6 * MIB),
        name="prepare",
    )(order, screen, pltpu.with_memory_space_constraint(integrals, pltpu.HBM))


def product(slabs, height, high_ref, low_ref):
    left = jnp.concatenate([piece[pl.ds(row, height), pl.ds(c * T, T)] for piece, row, c, place in slabs], axis=1)
    right = [jnp.concatenate([ref[pl.ds(s[3] * T, T), :] for s in slabs], axis=0) for ref in (high_ref, low_ref)]
    high, low = split(left)
    dot = functools.partial(jnp.dot, preferred_element_type=jnp.float32)
    two = dot(jnp.concatenate([high, low], axis=0), right[0])
    return two[:height] + (two[height:] + dot(high, right[1]))


def sums(blocks, work, pieces, high_ref, low_ref, emit):
    for (start, height), slabs in zip(blocks, work):
        slabs = [(pieces[i], row, c, place) for i, row, c, place in slabs]
        emit(start, height, product(slabs, height, high_ref, low_ref) if slabs else None)


def middle_kernel(blocks, work, n, first, *refs):
    pieces, (high_ref, low_ref), rest = refs[:n], refs[n : n + 2], refs[n + 2 :]
    total = rest[-1]

    def emit(start, height, value):
        rows = pl.ds(start, height)
        if value is not None:
            total[rows, :] = value if first else rest[0][rows, :] + value

    sums(blocks, work, pieces, high_ref, low_ref, emit)


def middle(blocks, pieces, work, high, low, totals, flops):
    width = high.shape[1]
    n = len(pieces)
    return pl.pallas_call(
        functools.partial(middle_kernel, blocks, work, n, not totals),
        out_shape=pltpu.VMEM((sum(height for _, height in blocks), width), jnp.float32),
        in_specs=whole(n + 2 + len(totals)),
        out_specs=whole(1)[0],
        input_output_aliases={n + 2 + i: i for i in range(len(totals))},
        compiler_params=pltpu.CompilerParams(vmem_limit_bytes=12 * MIB),
        cost_estimate=cost(flops),
        name="middle",
    )(*near((*pieces, high, low, *totals)))


def last_kernel(blocks, work, n, *refs):
    pieces, (high_ref, low_ref, total, weights_ref, zero_ref, ladder_ref, energy_ref) = refs[:n], refs[n:]
    energy_ref[...] = zero_ref[...]

    def emit(start, height, value):
        rows = pl.ds(start, height)
        value = 0.5 * (total[rows, :] if value is None else total[rows, :] + value)
        width = value.shape[1]
        ladder_ref[rows, :] = value
        terms = (weights_ref[rows, :] * value * value).reshape(height // 8, 8, width).sum(axis=0)
        energy_ref[...] += sum(terms[:, i * T : (i + 1) * T] for i in range(width // T))

    sums(blocks, work, pieces, high_ref, low_ref, emit)


def last(blocks, pieces, work, high, low, total, weights, zero):
    n = len(pieces)
    return pl.pallas_call(
        functools.partial(last_kernel, blocks, work, n),
        out_shape=[jax.ShapeDtypeStruct(weights.shape, jnp.float32), pltpu.VMEM((8, T), jnp.float32)],
        in_specs=whole(n + 5),
        out_specs=whole(2),
        compiler_params=pltpu.CompilerParams(vmem_limit_bytes=12 * MIB),
        name="last",
    )(*near((*pieces, high, low, total, weights, zero)))


ALL, INNER, OUTER, B0, B1, B2, B3 = (0, 1, 2, 3), (1, 2), (0, 3), (0,), (1,), (2,), (3,)
SENDS = {
    ("x", 1): (
        [(0, 0, ALL)],
        [(-1, 0, (0, 1)), (0, -1, INNER)],
        [(0, 1, INNER), (0, -2, INNER), (-1, -1, B1)],
        [(0, 2, INNER), (0, -3, INNER), (-1, 1, B1), (-1, -2, B1)],
        [(0, 3, INNER), (0, 4, B1), (-1, 2, B1), (-1, -3, B1)],
        [(0, 4, B2), (-1, 3, B1), (-1, 4, B1)],
    ),
    ("x", -1): (
        [(0, 0, ALL)],
        [(1, 0, (2, 3)), (0, -1, INNER), (0, 1, INNER)],
        [(0, -2, INNER), (0, 2, INNER), (1, -1, B2), (1, 1, B2)],
        [(0, -3, INNER), (0, 3, INNER), (1, -2, B2), (1, 2, B2)],
        [(0, 4, INNER), (1, -3, B2), (1, 3, B2)],
        [(1, 4, B2)],
    ),
    ("z", 1): (
        [(0, 0, ALL)],
        [(0, -1, ALL), (-1, 0, OUTER)],
        [(0, -2, ALL), (-1, -1, OUTER), (1, 0, OUTER), (2, 0, B0)],
        [(0, -3, (0, 1)), (-1, -2, OUTER), (1, -1, OUTER), (2, -1, B0), (2, 0, B3)],
        [(-1, -3, B0), (1, -2, OUTER), (2, -2, B0), (2, -1, B3)],
        [(1, -3, B0), (2, -3, B0), (2, -2, B3)],
    ),
    ("z", -1): (
        [(0, 0, ALL)],
        [(0, 1, ALL), (-1, 0, OUTER), (1, 0, OUTER)],
        [(0, 2, ALL), (-1, 1, OUTER), (1, 1, OUTER), (2, 0, OUTER)],
        [(0, 3, (2, 3)), (-1, 2, OUTER), (1, 2, OUTER), (2, 1, OUTER)],
        [(-1, 3, B3), (1, 3, B3), (2, 2, OUTER)],
        [(2, 3, B3)],
    ),
}


def wrap(value, size):
    return (value + size // 2 - 1) % size - size // 2 + 1


class Held:
    def __init__(self, blocks, own):
        self.blocks, self.where, self.fresh = blocks, {}, []
        self.put(own, [(0, 0, ALL)])

    def put(self, array, items):
        row = 0
        for dx, dz, members in items:
            for block in members:
                key = (wrap(dx, NX), wrap(dz, NZ), block)
                assert key not in self.where
                self.where[key] = (array, row)
                self.fresh.append(key)
                row += self.blocks[block][1]
        assert row == array.shape[0]

    def rows(self, items):
        runs = []
        for dx, dz, members in items:
            for block in members:
                array, row = self.where[dx, dz, block]
                height = self.blocks[block][1]
                if runs and runs[-1][0] is array and runs[-1][2] == row:
                    runs[-1][2] = row + height
                else:
                    runs.append([array, row, row + height])
        if len(runs) == 1:
            array, first, end = runs[0]
            return array if (first, end) == (0, array.shape[0]) else array[first:end]
        return pack(runs)

    def work(self):
        pieces, slabs = [], [[], [], [], []]
        for key in self.fresh:
            dx, dz, block = key
            array, row = self.where[key]
            number = [i for i, piece in enumerate(pieces) if piece is array]
            if not number:
                number = [len(pieces)]
                pieces.append(array)
            slabs[block].append((number[0], row, 0, ZPOS.index(dz) * NX + XPOS.index(dx)))
        self.fresh = []
        return pieces, slabs


def local(amplitudes, integrals, screen, slab_order, weights):
    count = amplitudes.shape[0]
    outer = count * 13 // 64
    inner = count // 2 - outer
    heights = (outer, inner, inner, outer)
    blocks = tuple((sum(heights[:i]), h) for i, h in enumerate(heights))
    me = lax.axis_index("col")
    x, z = me // NZ, me % NZ
    way = 1 - 2 * (lax.axis_index("row") % 2)
    xs = (x + way * jnp.array(XPOS)) % NX
    zs = (z + way * jnp.array(ZPOS)) % NZ
    order = slab_order[(zs[:, None] + xs[None, :] * NZ).reshape(-1)]

    line = Line(jnp.zeros((8, T), jnp.float32))
    held = Held(blocks, amplitudes)
    flying = {}
    totals = []

    def land(axis, d):
        array, items = flying.pop((axis, d))
        held.put(line.hold(array), items)

    def send(axis, d, k, first=()):
        items = SENDS[axis, d][k]
        rows = lax.optimization_barrier((*first, held.rows(items)))[-1] if first else held.rows(items)
        if k:
            rows = line.hold(rows)
        moved = [(dx - d * (axis == "x"), dz - d * (axis == "z"), members) for dx, dz, members in items]
        flying[axis, d] = shift(rows, axis, d), moved

    def multiply():
        pieces, slabs = held.work()
        totals[:] = [line.hold(middle(blocks, pieces, slabs, high, low, totals, 10**9))]

    for d in (1, -1):
        for axis in "xz":
            send(axis, d, 0, () if d == 1 else (order,))
    for k in range(1, len(SENDS["x", 1])):
        for d in (1, -1):
            if k < 3:
                land("x", d)
                land("z", d)
                send("z", d, k)
            else:
                land("z", d)
                send("z", d, k)
                line.tick(10**9 if k == 3 else 10**9)
                land("x", d)
            send("x", d, k)
            if k > 1:
                multiply()
        if k == 1:
            order, integrals = line.hold(order, integrals)
            high, low = line.hold(*prepare(order, screen, integrals))
            multiply()
    for d in (1, -1):
        land("z", d)
        land("x", d)
        if d == 1:
            multiply()
    assert len(held.where) == 4 * NX * NZ
    pieces, slabs = held.work()
    ladder, energy = last(blocks, pieces, slabs, high, low, *totals, weights, line.token)
    for axis in ("row", "col"):
        size = lax.axis_size(axis)
        energy = lax.all_to_all(jnp.broadcast_to(energy, (size, 8, T)), axis, 0, 0).sum(axis=0)
    cells = count * lax.axis_size("row") * weights.shape[1] * lax.axis_size("col")
    return ladder, jnp.sum(energy) / cells


def solution(mesh):
    return jax.shard_map(
        local,
        mesh=mesh,
        in_specs=(P("row", "col"), P(None, "col"), P(None, "col"), P(), P("row", "col")),
        out_specs=(P("row", "col"), P()),
        check_vma=False,
    )
```

time: 310 us -> 154 us (0.50)
  waiting for transfers between devices: 130 us -> 44.4 us
  matrix products: 58.1 us -> 0 us
  blocking collectives: 77.4 us -> 34.5 us
  starting transfers between devices: 0.04 us -> 40.3 us
  Pallas kernels: 0 us -> 28.9 us
  other arithmetic: 15.6 us -> 2.06 us
  between operations: 15.8 us -> 2.85 us
  local copies, waits for them, and re-layouts: 12.8 us -> 1.02 us
    all_gather x1 -> x0, waiting for transfers between devices: 129 us -> none  [local(): lax.all_gather(amplitudes, 'col', axis=1, tiled=True)]
    psum x1 -> x0, blocking collectives: 77.4 us -> none  [local(): lax.psum(jnp.sum(weights * ladder * ladder), ('row', 'col')) / all_cells]
    dot_general x1 -> x0, matrix products: 58.1 us -> none  [local(): jnp.dot(lax.all_gather(amplitudes, 'col', axis=1, tiled=True), placed, pr...]
    ppermute x0 -> x24, waiting for transfers between devices: none -> 44.4 us  [shift(): return lax.ppermute(v, ('row', 'col'), pairs)]
    ppermute x0 -> x24, starting transfers between devices: none -> 40.3 us  [shift(): return lax.ppermute(v, ('row', 'col'), pairs)]
    all_to_all x0 -> x2, blocking collectives: none -> 34.5 us  [local(): lax.all_to_all(jnp.broadcast_to(energy, (size, 8, T)), axis, 0, 0)]
    pallas_call x0 -> x35, Pallas kernels: none -> 28.9 us  [the longest x10 17.6 us: middle(): pl.pallas_call(functools.partial(middle_kernel, blocks, work, n, not tota...]
    mul x1, other arithmetic: 8.28 us -> 0.67 us  [local(): order = slab_order[(zs[:, None] + xs[None, :] * NZ).reshape(-1)]]
  transfers between devices with their start and end apart: 1 -> 24, of which waited for: 1 -> 10; matrix products, arithmetic and copies ran while one was open for 8% -> 2% of each run, Pallas kernels for 0% -> 17%
where the time goes in v1:
time: 154 us
  waiting for transfers between devices  44.4 us (29%)
  starting transfers between devices  40.3 us (26%)
  blocking collectives  34.5 us (22%)
  Pallas kernels  28.9 us (19%)
  between operations  2.85 us (2%)
  other arithmetic  2.06 us (1%)
    ppermute x24, waiting for transfers between devices, shift(): return lax.ppermute(v, ('row', 'col'), pairs)  44.4 us
    ppermute x24, starting transfers between devices, shift(): return lax.ppermute(v, ('row', 'col'), pairs)  40.3 us
    all_to_all x2, blocking collectives, local(): lax.all_to_all(jnp.broadcast_to(energy, (size, 8, T)), axis, 0, 0)  34.5 us
    pallas_call x10, Pallas kernels, middle(): pl.pallas_call(functools.partial(middle_kernel, blocks, work, n, not tota...  17.6 us
    pallas_call x1, Pallas kernels, prepare(): pl.pallas_call(prepare_kernel, out_shape=[pltpu.VMEM((depth, width), jnp....  4.59 us
    pallas_call x17, Pallas kernels, pack(): pl.pallas_call(functools.partial(pack_kernel, runs), out_shape=pltpu.VMEM...  4.59 us
  transfers between devices with their start and end apart: 24, of which 10 were waited for; matrix products, arithmetic and copies ran while one was open for 2% of the time, Pallas kernels for 17%

profile of v1, /device:TPU:1, one launch (start us, length us, event | category | flops | bytes accessed | tf_op | source)
XLA Modules:
  0.0 154.0 jit_solution(14908531605936101311)
XLA Ops:
  0.6 6.5 %collective-permute-start.1 = (f32[1024,128]{1,0:T(8,128)}, f32[1024,128]{1,0:T(8,128)S(1)}, u32[]{:S(2)}, u32[]{:S(2)}) collective-permute-start(f32[1024,128]{1,0:T(8,128)} %refs_0_.1), channel_id=1, source_target_pairs={{0,1},{1,2},{2,3},{3,4},{4,5},{5,6},{6,7},{7,0},{8,9},{9,10},{10,1... | collective-permute-start | bytes 1572872 | tf_op jit(solution)/shard_map/ppermute | solution.py:26
  7.1 2.5 %collective-permute-start = (f32[1024,128]{1,0:T(8,128)}, f32[1024,128]{1,0:T(8,128)S(1)}, u32[]{:S(2)}, u32[]{:S(2)}) collective-permute-start(f32[1024,128]{1,0:T(8,128)} %refs_0_.1), channel_id=1, source_target_pairs={{0,8},{1,9},{2,10},{3,11},{4,12},{5,13},{6,14},{7,15},{8,16},{9,17... | collective-permute-start | bytes 1572872 | tf_op jit(solution)/shard_map/ppermute | solution.py:26
  12.0 9.4 %collective-permute-done.refs_1_.refs_0_ = f32[1024,128]{1,0:T(8,128)S(1)} collective-permute-done((f32[1024,128]{1,0:T(8,128)}, f32[1024,128]{1,0:T(8,128)S(1)}, u32[]{:S(2)}, u32[]{:S(2)}) %collective-permute-start) | collective-permute-done | bytes 524320 | tf_op jit(solution)/shard_map/ppermute | solution.py:26
  23.3 3.3 %collective-permute-start.4 = (f32[1120,128]{1,0:T(8,128)}, f32[1120,128]{1,0:T(8,128)S(1)}, u32[]{:S(2)}, u32[]{:S(2)}) collective-permute-start(f32[1120,128]{1,0:T(8,128)} %pack.18), channel_id=1, source_target_pairs={{0,8},{1,9},{2,10},{3,11},{4,12},{5,13},{6,14},{7,15},{8,16},{9,17... | collective-permute-start | bytes 1720328 | tf_op jit(solution)/shard_map/ppermute | solution.py:26
  30.3 4.6 %prepare.1 = (bf16[4096,512]{1,0:T(8,128)(2,1)S(1)}, bf16[4096,512]{1,0:T(8,128)(2,1)S(1)}) custom-call(s32[32]{0:T(128)S(1)} %gather_fusion, s32[32,4]{1,0:T(8,128)S(1)} %copy.20.screen_ref, f32[4096,512]{1,0:T(8,128)} %b_ref), custom_call_target="tpu_custom_call" | custom-call | flops 1 | tf_op jit(solution)/shard_map/prepare/pallas_call | solution.py:121
  35.0 2.6 %middle.10.refs_4_ = f32[1024,512]{1,0:T(8,128)S(1)} custom-call(f32[1024,128]{1,0:T(8,128)S(1)} %copy-done.10, f32[1024,128]{1,0:T(8,128)S(1)} %copy-done.4, f32[1024,128]{1,0:T(8,128)S(1)} %copy-done.2, f32[1024,128]{1,0:T(8,128)S(1)} %copy-done.8, f32[1024,128]{1,0:T(8,128)S(1)} %copy-done.6, bf16[4096,512]{1,0:T(8,128)(2,1)S(1)} %get-tuple-element.140.refs_5_.refs_2_, ...), custom_call_target="tpu_custom_call" | custom-call | flops 1000000000 | tf_op jit(solution)/shard_map/middle/pallas_call | solution.py:163
  39.4 4.6 %collective-permute-start.9 = (f32[1520,128]{1,0:T(8,128)S(1)}, f32[1520,128]{1,0:T(8,128)S(1)}, u32[]{:S(2)}, u32[]{:S(2)}) collective-permute-start(f32[1520,128]{1,0:T(8,128)S(1)} %pack.22), channel_id=1, source_target_pairs={{0,8},{1,9},{2,10},{3,11},{4,12},{5,13},{6,14},{7,15},{8,16},{9,17... | collective-permute-start | bytes 2334728 | tf_op jit(solution)/shard_map/ppermute | solution.py:26
  47.0 1.9 %middle.12.refs_4_ = f32[1024,512]{1,0:T(8,128)S(1)} custom-call(f32[1728,128]{1,0:T(8,128)S(1)} %collective-permute-done.6.refs_2_.refs_0_.refs_1_, f32[1856,128]{1,0:T(8,128)S(1)} %collective-permute-done.7.refs_0_.refs_1_, bf16[4096,512]{1,0:T(8,128)(2,1)S(1)} %get-tuple-element.140.refs_5_.refs_2_, ...), custom_call_target="tpu_custom_call", output_to_operand_aliasing={{}: (4, {})} | custom-call | flops 1000000000 | tf_op jit(solution)/shard_map/middle/pallas_call | solution.py:163
  48.9 10.9 %collective-permute-done.8.refs_0_.refs_1_ = f32[2064,128]{1,0:T(8,128)S(1)} collective-permute-done((f32[2064,128]{1,0:T(8,128)S(1)}, f32[2064,128]{1,0:T(8,128)S(1)}, u32[]{:S(2)}, u32[]{:S(2)}) %collective-permute-start.8) | collective-permute-done | bytes 1056800 | tf_op jit(solution)/shard_map/ppermute | solution.py:26
  61.2 4.6 %collective-permute-start.13 = (f32[1824,128]{1,0:T(8,128)S(1)}, f32[1824,128]{1,0:T(8,128)S(1)}, u32[]{:S(2)}, u32[]{:S(2)}) collective-permute-start(f32[1824,128]{1,0:T(8,128)S(1)} %pack.26), channel_id=1, source_target_pairs={{0,8},{1,9},{2,10},{3,11},{4,12},{5,13},{6,14},{7,15},{8,16},{9,17... | collective-permute-start | bytes 2801672 | tf_op jit(solution)/shard_map/ppermute | solution.py:26
  65.8 1.9 %middle.13.refs_4_ = f32[1024,512]{1,0:T(8,128)S(1)} custom-call(f32[2064,128]{1,0:T(8,128)S(1)} %collective-permute-done.8.refs_0_.refs_1_, f32[1520,128]{1,0:T(8,128)S(1)} %collective-permute-done.9.refs_2_.refs_1_, bf16[4096,512]{1,0:T(8,128)(2,1)S(1)} %get-tuple-element.140.refs_5_.refs_2_, ...), custom_call_target="tpu_custom_call", output_to_operand_aliasing={{}: (4, {})} | custom-call | flops 1000000000 | tf_op jit(solution)/shard_map/middle/pallas_call | solution.py:163
  70.5 2.1 %middle.14.refs_4_ = f32[1024,512]{1,0:T(8,128)S(1)} custom-call(f32[2272,128]{1,0:T(8,128)S(1)} %collective-permute-done.10.refs_1_.refs_0_, f32[1824,128]{1,0:T(8,128)S(1)} %collective-permute-done.11.refs_2_.refs_1_, bf16[4096,512]{1,0:T(8,128)(2,1)S(1)} %get-tuple-element.140.refs_5_.refs_2_, ...), custom_call_target="tpu_custom_call", output_to_operand_aliasing={{}: (4, {})} | custom-call | flops 1000000000 | tf_op jit(solution)/shard_map/middle/pallas_call | solution.py:163
  72.6 5.7 %collective-permute-done.12.refs_0_.refs_1_ = f32[1760,128]{1,0:T(8,128)S(1)} collective-permute-done((f32[1760,128]{1,0:T(8,128)S(1)}, f32[1760,128]{1,0:T(8,128)S(1)}, u32[]{:S(2)}, u32[]{:S(2)}) %collective-permute-start.12) | collective-permute-done | bytes 901152 | tf_op jit(solution)/shard_map/ppermute | solution.py:26
  78.4 4.4 %collective-permute-start.17 = (f32[1520,128]{1,0:T(8,128)S(1)}, f32[1520,128]{1,0:T(8,128)S(1)}, u32[]{:S(2)}, u32[]{:S(2)}) collective-permute-start(f32[1520,128]{1,0:T(8,128)S(1)} %pack.29), channel_id=1, source_target_pairs={{0,8},{1,9},{2,10},{3,11},{4,12},{5,13},{6,14},{7,15},{8,16},{9,17... | collective-permute-start | bytes 2334728 | tf_op jit(solution)/shard_map/ppermute | solution.py:26
  86.0 1.9 %collective-permute-done.14.refs_0_.refs_1_ = f32[1760,128]{1,0:T(8,128)S(1)} collective-permute-done((f32[1760,128]{1,0:T(8,128)S(1)}, f32[1760,128]{1,0:T(8,128)S(1)}, u32[]{:S(2)}, u32[]{:S(2)}) %collective-permute-start.14) | collective-permute-done | bytes 901152 | tf_op jit(solution)/shard_map/ppermute | solution.py:26
  87.9 4.2 %collective-permute-done.15.refs_2_.refs_1_ = f32[1824,128]{1,0:T(8,128)S(1)} collective-permute-done((f32[1824,128]{1,0:T(8,128)S(1)}, f32[1824,128]{1,0:T(8,128)S(1)}, u32[]{:S(2)}, u32[]{:S(2)}) %collective-permute-start.15) | collective-permute-done | bytes 933920 | tf_op jit(solution)/shard_map/ppermute | solution.py:26
  92.3 2.5 %collective-permute-start.18 = (f32[832,128]{1,0:T(8,128)S(1)}, f32[832,128]{1,0:T(8,128)S(1)}, u32[]{:S(2)}, u32[]{:S(2)}) collective-permute-start(f32[832,128]{1,0:T(8,128)S(1)} %pack.30), channel_id=1, source_target_pairs={{0,7},{1,0},{2,1},{3,2},{4,3},{5,4},{6,5},{7,6},{8,15},{9,8},{10,9... | collective-permute-start | bytes 1277960 | tf_op jit(solution)/shard_map/ppermute | solution.py:26
  96.7 2.4 %collective-permute-start.21 = (f32[912,128]{1,0:T(8,128)S(1)}, f32[912,128]{1,0:T(8,128)S(1)}, u32[]{:S(2)}, u32[]{:S(2)}) collective-permute-start(f32[912,128]{1,0:T(8,128)S(1)} %pack.33), channel_id=1, source_target_pairs={{0,8},{1,9},{2,10},{3,11},{4,12},{5,13},{6,14},{7,15},{8,16},{9,17... | collective-permute-start | bytes 1400840 | tf_op jit(solution)/shard_map/ppermute | solution.py:26
  101.1 4.5 %collective-permute-done.18.refs_0_ = f32[832,128]{1,0:T(8,128)S(1)} collective-permute-done((f32[832,128]{1,0:T(8,128)S(1)}, f32[832,128]{1,0:T(8,128)S(1)}, u32[]{:S(2)}, u32[]{:S(2)}) %collective-permute-start.18) | collective-permute-done | bytes 426016 | tf_op jit(solution)/shard_map/ppermute | solution.py:26
  106.6 2.9 %collective-permute-done.19.refs_1_ = f32[1216,128]{1,0:T(8,128)S(1)} collective-permute-done((f32[1216,128]{1,0:T(8,128)S(1)}, f32[1216,128]{1,0:T(8,128)S(1)}, u32[]{:S(2)}, u32[]{:S(2)}) %collective-permute-start.19) | collective-permute-done | bytes 622624 | tf_op jit(solution)/shard_map/ppermute | solution.py:26
  112.1 2.8 %collective-permute-done.23.refs_1_ = f32[304,128]{1,0:T(8,128)S(1)} collective-permute-done((f32[304,128]{1,0:T(8,128)S(1)}, f32[304,128]{1,0:T(8,128)S(1)}, u32[]{:S(2)}, u32[]{:S(2)}) %collective-permute-start.23) | collective-permute-done | bytes 155680 | tf_op jit(solution)/shard_map/ppermute | solution.py:26
  114.9 2.2 %last.1 = (f32[1024,512]{1,0:T(8,128)}, f32[8,128]{1,0:T(8,128)S(1)}) custom-call(f32[208,128]{1,0:T(8,128)S(1)} %collective-permute-done.22.refs_0_, f32[304,128]{1,0:T(8,128)S(1)} %collective-permute-done.23.refs_1_, bf16[4096,512]{1,0:T(8,128)(2,1)S(1)} %get-tuple-element.140.refs_5_.refs_2_, bf16[4096,512]{1,0:T(8,128)(2,1)S(1)} %get-tuple-element.141.refs_6_.refs_3_, ...), custom_call_target="tpu_custom_call" | custom-call | tf_op jit(solution)/shard_map/last/pallas_call | solution.py:192
  117.1 16.0 %all_to_all.10 = f32[8,8,128]{2,1,0:T(8,128)S(1)} all-to-all(f32[8,8,128]{2,1,0:T(8,128)S(1)} %broadcast_in_dim.13), channel_id=1, replica_groups=mesh['row'=8,'col'=32] {'row'}, dimensions={0} | all-to-all | bytes 65536 | tf_op jit(solution)/shard_map/all_to_all | solution.py:353
  133.1 18.5 %all_to_all.11 = f32[32,8,128]{2,1,0:T(8,128)S(1)} all-to-all(f32[32,8,128]{2,1,0:T(8,128)S(1)} %broadcast_in_dim.14), channel_id=1, replica_groups=mesh['row'=8,'col'=32] {'col'}, dimensions={0} | all-to-all | bytes 262144 | tf_op jit(solution)/shard_map/all_to_all | solution.py:353
  (101 shorter events, 28.3 us)
Async XLA Ops:
  0.6 20.8 %collective-permute-start.1 = (f32[1024,128]{1,0:T(8,128)}, f32[1024,128]{1,0:T(8,128)S(1)}, u32[]{:S(2)}, u32[]{:S(2)}) collective-permute-start(f32[1024,128]{1,0:T(8,128)} %refs_0_.1), channel_id=1, source_target_pairs={{0,1},{1,2},{2,3},{3,4},{4,5},{5,6},{6,7},{7,0},{8,9},{9,10},{10,1... | collective-permute-start | bytes 1572872 | tf_op jit(solution)/shard_map/ppermute | solution.py:26
  7.1 14.3 %collective-permute-start = (f32[1024,128]{1,0:T(8,128)}, f32[1024,128]{1,0:T(8,128)S(1)}, u32[]{:S(2)}, u32[]{:S(2)}) collective-permute-start(f32[1024,128]{1,0:T(8,128)} %refs_0_.1), channel_id=1, source_target_pairs={{0,8},{1,9},{2,10},{3,11},{4,12},{5,13},{6,14},{7,15},{8,16},{9,17... | collective-permute-start | bytes 1572872 | tf_op jit(solution)/shard_map/ppermute | solution.py:26
  11.8 14.8 %collective-permute-start.2 = (f32[1024,128]{1,0:T(8,128)}, f32[1024,128]{1,0:T(8,128)S(1)}, u32[]{:S(2)}, u32[]{:S(2)}) collective-permute-start(f32[1024,128]{1,0:T(8,128)} %refs_0_.1), channel_id=1, source_target_pairs={{0,24},{1,25},{2,26},{3,27},{4,28},{5,29},{6,30},{7,31},{8,0},{9,1... | collective-permute-start | bytes 1572872 | tf_op jit(solution)/shard_map/ppermute | solution.py:26
  11.9 14.7 %collective-permute-start.3 = (f32[1024,128]{1,0:T(8,128)}, f32[1024,128]{1,0:T(8,128)S(1)}, u32[]{:S(2)}, u32[]{:S(2)}) collective-permute-start(f32[1024,128]{1,0:T(8,128)} %refs_0_.1), channel_id=1, source_target_pairs={{0,7},{1,0},{2,1},{3,2},{4,3},{5,4},{6,5},{7,6},{8,15},{9,8},{10,9... | collective-permute-start | bytes 1572872 | tf_op jit(solution)/shard_map/ppermute | solution.py:26
  22.4 15.6 %collective-permute-start.5 = (f32[1440,128]{1,0:T(8,128)}, f32[1440,128]{1,0:T(8,128)S(1)}, u32[]{:S(2)}, u32[]{:S(2)}) collective-permute-start(f32[1440,128]{1,0:T(8,128)} %pack.17), channel_id=1, source_target_pairs={{0,1},{1,2},{2,3},{3,4},{4,5},{5,6},{6,7},{7,0},{8,9},{9,10},{10,1... | collective-permute-start | bytes 2211848 | tf_op jit(solution)/shard_map/ppermute | solution.py:26
  23.3 14.3 %collective-permute-start.4 = (f32[1120,128]{1,0:T(8,128)}, f32[1120,128]{1,0:T(8,128)S(1)}, u32[]{:S(2)}, u32[]{:S(2)}) collective-permute-start(f32[1120,128]{1,0:T(8,128)} %pack.18), channel_id=1, source_target_pairs={{0,8},{1,9},{2,10},{3,11},{4,12},{5,13},{6,14},{7,15},{8,16},{9,17... | collective-permute-start | bytes 1720328 | tf_op jit(solution)/shard_map/ppermute | solution.py:26
  27.7 17.7 %collective-permute-start.7 = (f32[1856,128]{1,0:T(8,128)}, f32[1856,128]{1,0:T(8,128)S(1)}, u32[]{:S(2)}, u32[]{:S(2)}) collective-permute-start(f32[1856,128]{1,0:T(8,128)} %pack.19), channel_id=1, source_target_pairs={{0,7},{1,0},{2,1},{3,2},{4,3},{5,4},{6,5},{7,6},{8,15},{9,8},{10,9... | collective-permute-start | bytes 2850824 | tf_op jit(solution)/shard_map/ppermute | solution.py:26
  30.2 15.3 %collective-permute-start.6 = (f32[1728,128]{1,0:T(8,128)}, f32[1728,128]{1,0:T(8,128)S(1)}, u32[]{:S(2)}, u32[]{:S(2)}) collective-permute-start(f32[1728,128]{1,0:T(8,128)} %pack.20), channel_id=1, source_target_pairs={{0,24},{1,25},{2,26},{3,27},{4,28},{5,29},{6,30},{7,31},{8,0},{9,1... | collective-permute-start | bytes 2654216 | tf_op jit(solution)/shard_map/ppermute | solution.py:26
  38.1 21.7 %collective-permute-start.8 = (f32[2064,128]{1,0:T(8,128)S(1)}, f32[2064,128]{1,0:T(8,128)S(1)}, u32[]{:S(2)}, u32[]{:S(2)}) collective-permute-start(f32[2064,128]{1,0:T(8,128)S(1)} %pack.21), channel_id=1, source_target_pairs={{0,1},{1,2},{2,3},{3,4},{4,5},{5,6},{6,7},{7,0},{8,9},{9,10},{10,1... | collective-permute-start | bytes 3170312 | tf_op jit(solution)/shard_map/ppermute | solution.py:26
  39.4 21.7 %collective-permute-start.9 = (f32[1520,128]{1,0:T(8,128)S(1)}, f32[1520,128]{1,0:T(8,128)S(1)}, u32[]{:S(2)}, u32[]{:S(2)}) collective-permute-start(f32[1520,128]{1,0:T(8,128)S(1)} %pack.22), channel_id=1, source_target_pairs={{0,8},{1,9},{2,10},{3,11},{4,12},{5,13},{6,14},{7,15},{8,16},{9,17... | collective-permute-start | bytes 2334728 | tf_op jit(solution)/shard_map/ppermute | solution.py:26
  45.6 23.7 %collective-permute-start.10 = (f32[2272,128]{1,0:T(8,128)S(1)}, f32[2272,128]{1,0:T(8,128)S(1)}, u32[]{:S(2)}, u32[]{:S(2)}) collective-permute-start(f32[2272,128]{1,0:T(8,128)S(1)} %pack.23), channel_id=1, source_target_pairs={{0,7},{1,0},{2,1},{3,2},{4,3},{5,4},{6,5},{7,6},{8,15},{9,8},{10,9... | collective-permute-start | bytes 3489800 | tf_op jit(solution)/shard_map/ppermute | solution.py:26
  46.7 23.6 %collective-permute-start.11 = (f32[1824,128]{1,0:T(8,128)S(1)}, f32[1824,128]{1,0:T(8,128)S(1)}, u32[]{:S(2)}, u32[]{:S(2)}) collective-permute-start(f32[1824,128]{1,0:T(8,128)S(1)} %pack.24), channel_id=1, source_target_pairs={{0,24},{1,25},{2,26},{3,27},{4,28},{5,29},{6,30},{7,31},{8,0},{9,1... | collective-permute-start | bytes 2801672 | tf_op jit(solution)/shard_map/ppermute | solution.py:26
  59.9 18.4 %collective-permute-start.12 = (f32[1760,128]{1,0:T(8,128)S(1)}, f32[1760,128]{1,0:T(8,128)S(1)}, u32[]{:S(2)}, u32[]{:S(2)}) collective-permute-start(f32[1760,128]{1,0:T(8,128)S(1)} %pack.25), channel_id=1, source_target_pairs={{0,1},{1,2},{2,3},{3,4},{4,5},{5,6},{6,7},{7,0},{8,9},{9,10},{10,1... | collective-permute-start | bytes 2703368 | tf_op jit(solution)/shard_map/ppermute | solution.py:26
  61.2 17.2 %collective-permute-start.13 = (f32[1824,128]{1,0:T(8,128)S(1)}, f32[1824,128]{1,0:T(8,128)S(1)}, u32[]{:S(2)}, u32[]{:S(2)}) collective-permute-start(f32[1824,128]{1,0:T(8,128)S(1)} %pack.26), channel_id=1, source_target_pairs={{0,8},{1,9},{2,10},{3,11},{4,12},{5,13},{6,14},{7,15},{8,16},{9,17... | collective-permute-start | bytes 2801672 | tf_op jit(solution)/shard_map/ppermute | solution.py:26
  69.3 18.6 %collective-permute-start.14 = (f32[1760,128]{1,0:T(8,128)S(1)}, f32[1760,128]{1,0:T(8,128)S(1)}, u32[]{:S(2)}, u32[]{:S(2)}) collective-permute-start(f32[1760,128]{1,0:T(8,128)S(1)} %slice.9), channel_id=1, source_target_pairs={{0,7},{1,0},{2,1},{3,2},{4,3},{5,4},{6,5},{7,6},{8,15},{9,8},{10,9... | collective-permute-start | bytes 2703368 | tf_op jit(solution)/shard_map/ppermute | solution.py:26
  70.4 21.7 %collective-permute-start.15 = (f32[1824,128]{1,0:T(8,128)S(1)}, f32[1824,128]{1,0:T(8,128)S(1)}, u32[]{:S(2)}, u32[]{:S(2)}) collective-permute-start(f32[1824,128]{1,0:T(8,128)S(1)} %pack.27), channel_id=1, source_target_pairs={{0,24},{1,25},{2,26},{3,27},{4,28},{5,29},{6,30},{7,31},{8,0},{9,1... | collective-permute-start | bytes 2801672 | tf_op jit(solution)/shard_map/ppermute | solution.py:26
  78.4 18.3 %collective-permute-start.17 = (f32[1520,128]{1,0:T(8,128)S(1)}, f32[1520,128]{1,0:T(8,128)S(1)}, u32[]{:S(2)}, u32[]{:S(2)}) collective-permute-start(f32[1520,128]{1,0:T(8,128)S(1)} %pack.29), channel_id=1, source_target_pairs={{0,8},{1,9},{2,10},{3,11},{4,12},{5,13},{6,14},{7,15},{8,16},{9,17... | collective-permute-start | bytes 2334728 | tf_op jit(solution)/shard_map/ppermute | solution.py:26
  82.8 13.8 %collective-permute-start.16 = (f32[1040,128]{1,0:T(8,128)S(1)}, f32[1040,128]{1,0:T(8,128)S(1)}, u32[]{:S(2)}, u32[]{:S(2)}) collective-permute-start(f32[1040,128]{1,0:T(8,128)S(1)} %pack.28), channel_id=1, source_target_pairs={{0,1},{1,2},{2,3},{3,4},{4,5},{5,6},{6,7},{7,0},{8,9},{9,10},{10,1... | collective-permute-start | bytes 1597448 | tf_op jit(solution)/shard_map/ppermute | solution.py:26
  92.2 17.3 %collective-permute-start.19 = (f32[1216,128]{1,0:T(8,128)S(1)}, f32[1216,128]{1,0:T(8,128)S(1)}, u32[]{:S(2)}, u32[]{:S(2)}) collective-permute-start(f32[1216,128]{1,0:T(8,128)S(1)} %pack.31), channel_id=1, source_target_pairs={{0,24},{1,25},{2,26},{3,27},{4,28},{5,29},{6,30},{7,31},{8,0},{9,1... | collective-permute-start | bytes 1867784 | tf_op jit(solution)/shard_map/ppermute | solution.py:26
  92.3 13.4 %collective-permute-start.18 = (f32[832,128]{1,0:T(8,128)S(1)}, f32[832,128]{1,0:T(8,128)S(1)}, u32[]{:S(2)}, u32[]{:S(2)}) collective-permute-start(f32[832,128]{1,0:T(8,128)S(1)} %pack.30), channel_id=1, source_target_pairs={{0,7},{1,0},{2,1},{3,2},{4,3},{5,4},{6,5},{7,6},{8,15},{9,8},{10,9... | collective-permute-start | bytes 1277960 | tf_op jit(solution)/shard_map/ppermute | solution.py:26
  96.7 14.3 %collective-permute-start.21 = (f32[912,128]{1,0:T(8,128)S(1)}, f32[912,128]{1,0:T(8,128)S(1)}, u32[]{:S(2)}, u32[]{:S(2)}) collective-permute-start(f32[912,128]{1,0:T(8,128)S(1)} %pack.33), channel_id=1, source_target_pairs={{0,8},{1,9},{2,10},{3,11},{4,12},{5,13},{6,14},{7,15},{8,16},{9,17... | collective-permute-start | bytes 1400840 | tf_op jit(solution)/shard_map/ppermute | solution.py:26
  99.2 11.9 %collective-permute-start.20 = (f32[624,128]{1,0:T(8,128)S(1)}, f32[624,128]{1,0:T(8,128)S(1)}, u32[]{:S(2)}, u32[]{:S(2)}) collective-permute-start(f32[624,128]{1,0:T(8,128)S(1)} %pack.32), channel_id=1, source_target_pairs={{0,1},{1,2},{2,3},{3,4},{4,5},{5,6},{6,7},{7,0},{8,9},{9,10},{10,1... | collective-permute-start | bytes 958472 | tf_op jit(solution)/shard_map/ppermute | solution.py:26
  105.6 6.5 %collective-permute-start.22 = (f32[208,128]{1,0:T(8,128)S(1)}, f32[208,128]{1,0:T(8,128)S(1)}, u32[]{:S(2)}, u32[]{:S(2)}) collective-permute-start(f32[208,128]{1,0:T(8,128)S(1)} %slice.10), channel_id=1, source_target_pairs={{0,7},{1,0},{2,1},{3,2},{4,3},{5,4},{6,5},{7,6},{8,15},{9,8},{10,9... | collective-permute-start | bytes 319496 | tf_op jit(solution)/shard_map/ppermute | solution.py:26
  109.5 5.4 %collective-permute-start.23 = (f32[304,128]{1,0:T(8,128)S(1)}, f32[304,128]{1,0:T(8,128)S(1)}, u32[]{:S(2)}, u32[]{:S(2)}) collective-permute-start(f32[304,128]{1,0:T(8,128)S(1)} %slice.11), channel_id=1, source_target_pairs={{0,24},{1,25},{2,26},{3,27},{4,28},{5,29},{6,30},{7,31},{8,0},{9,1... | collective-permute-start | bytes 466952 | tf_op jit(solution)/shard_map/ppermute | solution.py:26
  (12 other events, 64.5 us)

commit v2 on v1

--- a/solution.py
+++ b/solution.py
@@ -322,6 +322,8 @@
     for d in (1, -1):
         for axis in "xz":
             send(axis, d, 0, () if d == 1 else (order,))
+    order, integrals = line.hold(order, integrals)
+    high, low = line.hold(*prepare(order, screen, integrals))
     for k in range(1, len(SENDS["x", 1])):
         for d in (1, -1):
             if k < 3:
@@ -334,11 +336,6 @@
                 line.tick(10**9 if k == 3 else 10**9)
                 land("x", d)
             send("x", d, k)
-            if k > 1:
-                multiply()
-        if k == 1:
-            order, integrals = line.hold(order, integrals)
-            high, low = line.hold(*prepare(order, screen, integrals))
             multiply()
     for d in (1, -1):
         land("z", d)

time: 154 us -> 153 us (level)
  Pallas kernels: 28.9 us -> 25.4 us
  waiting for transfers between devices: 44.4 us -> 46.7 us
    pallas_call x17, Pallas kernels: 4.59 us -> 0.86 us  [pack(): pl.pallas_call(functools.partial(pack_kernel, runs), out_shape=pltpu.VMEM...]
    ppermute x24, waiting for transfers between devices: 44.4 us -> 46.7 us  [shift(): return lax.ppermute(v, ('row', 'col'), pairs)]
    pallas_call x10 -> x11, Pallas kernels: 17.6 us -> 17.8 us  [middle(): pl.pallas_call(functools.partial(middle_kernel, blocks, work, n, not tota...]
  transfers between devices with their start and end apart: 24 -> 24, of which waited for: 10 -> 12; matrix products, arithmetic and copies ran while one was open for 2% -> 2% of each run, Pallas kernels for 17% -> 15%
where the time goes in v2:
time: 153 us
  waiting for transfers between devices  46.7 us (31%)
  starting transfers between devices  39.4 us (26%)
  blocking collectives  34.6 us (23%)
  Pallas kernels  25.4 us (17%)
  between operations  2.84 us (2%)
  other arithmetic  2.06 us (1%)
  local copies, waits for them, and re-layouts  1.66 us (1%)
    ppermute x24, waiting for transfers between devices, shift(): return lax.ppermute(v, ('row', 'col'), pairs)  46.7 us
    ppermute x24, starting transfers between devices, shift(): return lax.ppermute(v, ('row', 'col'), pairs)  39.4 us
    all_to_all x2, blocking collectives, local(): lax.all_to_all(jnp.broadcast_to(energy, (size, 8, T)), axis, 0, 0)  34.6 us
    pallas_call x11, Pallas kernels, middle(): pl.pallas_call(functools.partial(middle_kernel, blocks, work, n, not tota...  17.8 us
    pallas_call x1, Pallas kernels, prepare(): pl.pallas_call(prepare_kernel, out_shape=[pltpu.VMEM((depth, width), jnp....  4.59 us
  transfers between devices with their start and end apart: 24, of which 12 were waited for; matrix products, arithmetic and copies ran while one was open for 2% of the time, Pallas kernels for 15%

profile of v2, /device:TPU:1, one launch (start us, length us, event | category | flops | bytes accessed | tf_op | source)
XLA Modules:
  0.0 152.7 jit_solution(6643642426701774739)
XLA Ops:
  0.6 6.5 %collective-permute-start.1 = (f32[1024,128]{1,0:T(8,128)}, f32[1024,128]{1,0:T(8,128)S(1)}, u32[]{:S(2)}, u32[]{:S(2)}) collective-permute-start(f32[1024,128]{1,0:T(8,128)} %refs_0_.1), channel_id=1, source_target_pairs={{0,1},{1,2},{2,3},{3,4},{4,5},{5,6},{6,7},{7,0},{8,9},{9,10},{10,1... | collective-permute-start | bytes 1572872 | tf_op jit(solution)/shard_map/ppermute | solution.py:26
  7.1 2.5 %collective-permute-start = (f32[1024,128]{1,0:T(8,128)}, f32[1024,128]{1,0:T(8,128)S(1)}, u32[]{:S(2)}, u32[]{:S(2)}) collective-permute-start(f32[1024,128]{1,0:T(8,128)} %refs_0_.1), channel_id=1, source_target_pairs={{0,8},{1,9},{2,10},{3,11},{4,12},{5,13},{6,14},{7,15},{8,16},{9,17... | collective-permute-start | bytes 1572872 | tf_op jit(solution)/shard_map/ppermute | solution.py:26
  12.8 4.6 %prepare.1 = (bf16[4096,512]{1,0:T(8,128)(2,1)S(1)}, bf16[4096,512]{1,0:T(8,128)(2,1)S(1)}) custom-call(s32[32]{0:T(128)S(1)} %gather_fusion, s32[32,4]{1,0:T(8,128)S(1)} %copy.21.screen_ref, f32[4096,512]{1,0:T(8,128)} %b_ref), custom_call_target="tpu_custom_call" | custom-call | flops 1 | tf_op jit(solution)/shard_map/prepare/pallas_call | solution.py:121
  17.4 4.1 %collective-permute-done.refs_1_.refs_0_ = f32[1024,128]{1,0:T(8,128)S(1)} collective-permute-done((f32[1024,128]{1,0:T(8,128)}, f32[1024,128]{1,0:T(8,128)S(1)}, u32[]{:S(2)}, u32[]{:S(2)}) %collective-permute-start) | collective-permute-done | bytes 524320 | tf_op jit(solution)/shard_map/ppermute | solution.py:26
  21.6 3.4 %collective-permute-start.4 = (f32[1120,128]{1,0:T(8,128)S(1)}, f32[1120,128]{1,0:T(8,128)S(1)}, u32[]{:S(2)}, u32[]{:S(2)}) collective-permute-start(f32[1120,128]{1,0:T(8,128)S(1)} %pack.18), channel_id=1, source_target_pairs={{0,8},{1,9},{2,10},{3,11},{4,12},{5,13},{6,14},{7,15},{8,16},{9,17... | collective-permute-start | bytes 1720328 | tf_op jit(solution)/shard_map/ppermute | solution.py:26
  29.6 5.0 %collective-permute-done.4.refs_2_.refs_0_.refs_1_ = f32[1120,128]{1,0:T(8,128)S(1)} collective-permute-done((f32[1120,128]{1,0:T(8,128)S(1)}, f32[1120,128]{1,0:T(8,128)S(1)}, u32[]{:S(2)}, u32[]{:S(2)}) %collective-permute-start.4) | collective-permute-done | bytes 573472 | tf_op jit(solution)/shard_map/ppermute | solution.py:26
  34.6 2.2 %collective-permute-done.5.refs_0_.refs_1_ = f32[1440,128]{1,0:T(8,128)S(1)} collective-permute-done((f32[1440,128]{1,0:T(8,128)S(1)}, f32[1440,128]{1,0:T(8,128)S(1)}, u32[]{:S(2)}, u32[]{:S(2)}) %collective-permute-start.5) | collective-permute-done | bytes 737312 | tf_op jit(solution)/shard_map/ppermute | solution.py:26
  38.0 4.4 %collective-permute-start.9 = (f32[1520,128]{1,0:T(8,128)S(1)}, f32[1520,128]{1,0:T(8,128)S(1)}, u32[]{:S(2)}, u32[]{:S(2)}) collective-permute-start(f32[1520,128]{1,0:T(8,128)S(1)} %pack.22), channel_id=1, source_target_pairs={{0,8},{1,9},{2,10},{3,11},{4,12},{5,13},{6,14},{7,15},{8,16},{9,17... | collective-permute-start | bytes 2334728 | tf_op jit(solution)/shard_map/ppermute | solution.py:26
  48.4 10.2 %collective-permute-done.8.refs_0_.refs_1_ = f32[2064,128]{1,0:T(8,128)S(1)} collective-permute-done((f32[2064,128]{1,0:T(8,128)S(1)}, f32[2064,128]{1,0:T(8,128)S(1)}, u32[]{:S(2)}, u32[]{:S(2)}) %collective-permute-start.8) | collective-permute-done | bytes 1056800 | tf_op jit(solution)/shard_map/ppermute | solution.py:26
  59.8 4.4 %collective-permute-start.13 = (f32[1824,128]{1,0:T(8,128)S(1)}, f32[1824,128]{1,0:T(8,128)S(1)}, u32[]{:S(2)}, u32[]{:S(2)}) collective-permute-start(f32[1824,128]{1,0:T(8,128)S(1)} %pack.26), channel_id=1, source_target_pairs={{0,8},{1,9},{2,10},{3,11},{4,12},{5,13},{6,14},{7,15},{8,16},{9,17... | collective-permute-start | bytes 2801672 | tf_op jit(solution)/shard_map/ppermute | solution.py:26
  64.2 1.9 %middle.15.refs_4_ = f32[1024,512]{1,0:T(8,128)S(1)} custom-call(f32[2064,128]{1,0:T(8,128)S(1)} %collective-permute-done.8.refs_0_.refs_1_, f32[1520,128]{1,0:T(8,128)S(1)} %collective-permute-done.9.refs_2_.refs_1_, bf16[4096,512]{1,0:T(8,128)(2,1)S(1)} %get-tuple-element.135.refs_3_.refs_2_, ...), custom_call_target="tpu_custom_call", output_to_operand_aliasing={{}: (4, {})} | custom-call | flops 1000000000 | tf_op jit(solution)/shard_map/middle/pallas_call | solution.py:163
  66.0 3.1 %collective-permute-done.10.refs_1_.refs_0_ = f32[2272,128]{1,0:T(8,128)S(1)} collective-permute-done((f32[2272,128]{1,0:T(8,128)S(1)}, f32[2272,128]{1,0:T(8,128)S(1)}, u32[]{:S(2)}, u32[]{:S(2)}) %collective-permute-start.10) | collective-permute-done | bytes 1163296 | tf_op jit(solution)/shard_map/ppermute | solution.py:26
  69.5 2.1 %middle.16.refs_4_ = f32[1024,512]{1,0:T(8,128)S(1)} custom-call(f32[2272,128]{1,0:T(8,128)S(1)} %collective-permute-done.10.refs_1_.refs_0_, f32[1824,128]{1,0:T(8,128)S(1)} %collective-permute-done.11.refs_2_.refs_1_, bf16[4096,512]{1,0:T(8,128)(2,1)S(1)} %get-tuple-element.135.refs_3_.refs_2_, ...), custom_call_target="tpu_custom_call", output_to_operand_aliasing={{}: (4, {})} | custom-call | flops 1000000000 | tf_op jit(solution)/shard_map/middle/pallas_call | solution.py:163
  71.6 5.5 %collective-permute-done.12.refs_0_.refs_1_ = f32[1760,128]{1,0:T(8,128)S(1)} collective-permute-done((f32[1760,128]{1,0:T(8,128)S(1)}, f32[1760,128]{1,0:T(8,128)S(1)}, u32[]{:S(2)}, u32[]{:S(2)}) %collective-permute-start.12) | collective-permute-done | bytes 901152 | tf_op jit(solution)/shard_map/ppermute | solution.py:26
  77.2 5.2 %collective-permute-start.17 = (f32[1520,128]{1,0:T(8,128)S(1)}, f32[1520,128]{1,0:T(8,128)S(1)}, u32[]{:S(2)}, u32[]{:S(2)}) collective-permute-start(f32[1520,128]{1,0:T(8,128)S(1)} %pack.29), channel_id=1, source_target_pairs={{0,8},{1,9},{2,10},{3,11},{4,12},{5,13},{6,14},{7,15},{8,16},{9,17... | collective-permute-start | bytes 2334728 | tf_op jit(solution)/shard_map/ppermute | solution.py:26
  85.9 4.2 %collective-permute-done.15.refs_2_.refs_1_ = f32[1824,128]{1,0:T(8,128)S(1)} collective-permute-done((f32[1824,128]{1,0:T(8,128)S(1)}, f32[1824,128]{1,0:T(8,128)S(1)}, u32[]{:S(2)}, u32[]{:S(2)}) %collective-permute-start.15) | collective-permute-done | bytes 933920 | tf_op jit(solution)/shard_map/ppermute | solution.py:26
  90.3 3.3 %collective-permute-start.18 = (f32[832,128]{1,0:T(8,128)S(1)}, f32[832,128]{1,0:T(8,128)S(1)}, u32[]{:S(2)}, u32[]{:S(2)}) collective-permute-start(f32[832,128]{1,0:T(8,128)S(1)} %pack.30), channel_id=1, source_target_pairs={{0,7},{1,0},{2,1},{3,2},{4,3},{5,4},{6,5},{7,6},{8,15},{9,8},{10,9... | collective-permute-start | bytes 1277960 | tf_op jit(solution)/shard_map/ppermute | solution.py:26
  95.5 2.4 %collective-permute-start.21 = (f32[912,128]{1,0:T(8,128)S(1)}, f32[912,128]{1,0:T(8,128)S(1)}, u32[]{:S(2)}, u32[]{:S(2)}) collective-permute-start(f32[912,128]{1,0:T(8,128)S(1)} %pack.33), channel_id=1, source_target_pairs={{0,8},{1,9},{2,10},{3,11},{4,12},{5,13},{6,14},{7,15},{8,16},{9,17... | collective-permute-start | bytes 1400840 | tf_op jit(solution)/shard_map/ppermute | solution.py:26
  99.4 3.5 %collective-permute-done.18.refs_0_ = f32[832,128]{1,0:T(8,128)S(1)} collective-permute-done((f32[832,128]{1,0:T(8,128)S(1)}, f32[832,128]{1,0:T(8,128)S(1)}, u32[]{:S(2)}, u32[]{:S(2)}) %collective-permute-start.18) | collective-permute-done | bytes 426016 | tf_op jit(solution)/shard_map/ppermute | solution.py:26
  104.8 2.2 %collective-permute-done.19.refs_1_ = f32[1216,128]{1,0:T(8,128)S(1)} collective-permute-done((f32[1216,128]{1,0:T(8,128)S(1)}, f32[1216,128]{1,0:T(8,128)S(1)}, u32[]{:S(2)}, u32[]{:S(2)}) %collective-permute-start.19) | collective-permute-done | bytes 622624 | tf_op jit(solution)/shard_map/ppermute | solution.py:26
  109.6 3.9 %collective-permute-done.23.refs_1_ = f32[304,128]{1,0:T(8,128)S(1)} collective-permute-done((f32[304,128]{1,0:T(8,128)S(1)}, f32[304,128]{1,0:T(8,128)S(1)}, u32[]{:S(2)}, u32[]{:S(2)}) %collective-permute-start.23) | collective-permute-done | bytes 155680 | tf_op jit(solution)/shard_map/ppermute | solution.py:26
  113.5 2.2 %last.1 = (f32[1024,512]{1,0:T(8,128)}, f32[8,128]{1,0:T(8,128)S(1)}) custom-call(f32[208,128]{1,0:T(8,128)S(1)} %collective-permute-done.22.refs_0_, f32[304,128]{1,0:T(8,128)S(1)} %collective-permute-done.23.refs_1_, bf16[4096,512]{1,0:T(8,128)(2,1)S(1)} %get-tuple-element.135.refs_3_.refs_2_, bf16[4096,512]{1,0:T(8,128)(2,1)S(1)} %get-tuple-element.136.refs_4_.refs_3_, ...), custom_call_target="tpu_custom_call" | custom-call | tf_op jit(solution)/shard_map/last/pallas_call | solution.py:192
  115.7 16.1 %all_to_all.10 = f32[8,8,128]{2,1,0:T(8,128)S(1)} all-to-all(f32[8,8,128]{2,1,0:T(8,128)S(1)} %broadcast_in_dim.13), channel_id=1, replica_groups=mesh['row'=8,'col'=32] {'row'}, dimensions={0} | all-to-all | bytes 65536 | tf_op jit(solution)/shard_map/all_to_all | solution.py:350
  131.8 18.4 %all_to_all.11 = f32[32,8,128]{2,1,0:T(8,128)S(1)} all-to-all(f32[32,8,128]{2,1,0:T(8,128)S(1)} %broadcast_in_dim.14), channel_id=1, replica_groups=mesh['row'=8,'col'=32] {'col'}, dimensions={0} | all-to-all | bytes 262144 | tf_op jit(solution)/shard_map/all_to_all | solution.py:350
  (84 shorter events, 28.5 us)
Async XLA Ops:
  0.6 20.8 %collective-permute-start.1 = (f32[1024,128]{1,0:T(8,128)}, f32[1024,128]{1,0:T(8,128)S(1)}, u32[]{:S(2)}, u32[]{:S(2)}) collective-permute-start(f32[1024,128]{1,0:T(8,128)} %refs_0_.1), channel_id=1, source_target_pairs={{0,1},{1,2},{2,3},{3,4},{4,5},{5,6},{6,7},{7,0},{8,9},{9,10},{10,1... | collective-permute-start | bytes 1572872 | tf_op jit(solution)/shard_map/ppermute | solution.py:26
  7.1 14.3 %collective-permute-start = (f32[1024,128]{1,0:T(8,128)}, f32[1024,128]{1,0:T(8,128)S(1)}, u32[]{:S(2)}, u32[]{:S(2)}) collective-permute-start(f32[1024,128]{1,0:T(8,128)} %refs_0_.1), channel_id=1, source_target_pairs={{0,8},{1,9},{2,10},{3,11},{4,12},{5,13},{6,14},{7,15},{8,16},{9,17... | collective-permute-start | bytes 1572872 | tf_op jit(solution)/shard_map/ppermute | solution.py:26
  11.8 15.0 %collective-permute-start.2 = (f32[1024,128]{1,0:T(8,128)}, f32[1024,128]{1,0:T(8,128)S(1)}, u32[]{:S(2)}, u32[]{:S(2)}) collective-permute-start(f32[1024,128]{1,0:T(8,128)} %refs_0_.1), channel_id=1, source_target_pairs={{0,24},{1,25},{2,26},{3,27},{4,28},{5,29},{6,30},{7,31},{8,0},{9,1... | collective-permute-start | bytes 1572872 | tf_op jit(solution)/shard_map/ppermute | solution.py:26
  11.9 14.9 %collective-permute-start.3 = (f32[1024,128]{1,0:T(8,128)}, f32[1024,128]{1,0:T(8,128)S(1)}, u32[]{:S(2)}, u32[]{:S(2)}) collective-permute-start(f32[1024,128]{1,0:T(8,128)} %refs_0_.1), channel_id=1, source_target_pairs={{0,7},{1,0},{2,1},{3,2},{4,3},{5,4},{6,5},{7,6},{8,15},{9,8},{10,9... | collective-permute-start | bytes 1572872 | tf_op jit(solution)/shard_map/ppermute | solution.py:26
  21.5 15.4 %collective-permute-start.5 = (f32[1440,128]{1,0:T(8,128)S(1)}, f32[1440,128]{1,0:T(8,128)S(1)}, u32[]{:S(2)}, u32[]{:S(2)}) collective-permute-start(f32[1440,128]{1,0:T(8,128)S(1)} %pack.17), channel_id=1, source_target_pairs={{0,1},{1,2},{2,3},{3,4},{4,5},{5,6},{6,7},{7,0},{8,9},{9,10},{10,1... | collective-permute-start | bytes 2211848 | tf_op jit(solution)/shard_map/ppermute | solution.py:26
  21.6 13.0 %collective-permute-start.4 = (f32[1120,128]{1,0:T(8,128)S(1)}, f32[1120,128]{1,0:T(8,128)S(1)}, u32[]{:S(2)}, u32[]{:S(2)}) collective-permute-start(f32[1120,128]{1,0:T(8,128)S(1)} %pack.18), channel_id=1, source_target_pairs={{0,8},{1,9},{2,10},{3,11},{4,12},{5,13},{6,14},{7,15},{8,16},{9,17... | collective-permute-start | bytes 1720328 | tf_op jit(solution)/shard_map/ppermute | solution.py:26
  26.9 18.2 %collective-permute-start.7 = (f32[1856,128]{1,0:T(8,128)S(1)}, f32[1856,128]{1,0:T(8,128)S(1)}, u32[]{:S(2)}, u32[]{:S(2)}) collective-permute-start(f32[1856,128]{1,0:T(8,128)S(1)} %pack.19), channel_id=1, source_target_pairs={{0,7},{1,0},{2,1},{3,2},{4,3},{5,4},{6,5},{7,6},{8,15},{9,8},{10,9... | collective-permute-start | bytes 2850824 | tf_op jit(solution)/shard_map/ppermute | solution.py:26
  28.5 15.4 %collective-permute-start.6 = (f32[1728,128]{1,0:T(8,128)S(1)}, f32[1728,128]{1,0:T(8,128)S(1)}, u32[]{:S(2)}, u32[]{:S(2)}) collective-permute-start(f32[1728,128]{1,0:T(8,128)S(1)} %pack.20), channel_id=1, source_target_pairs={{0,24},{1,25},{2,26},{3,27},{4,28},{5,29},{6,30},{7,31},{8,0},{9,1... | collective-permute-start | bytes 2654216 | tf_op jit(solution)/shard_map/ppermute | solution.py:26
  36.9 21.7 %collective-permute-start.8 = (f32[2064,128]{1,0:T(8,128)S(1)}, f32[2064,128]{1,0:T(8,128)S(1)}, u32[]{:S(2)}, u32[]{:S(2)}) collective-permute-start(f32[2064,128]{1,0:T(8,128)S(1)} %pack.21), channel_id=1, source_target_pairs={{0,1},{1,2},{2,3},{3,4},{4,5},{5,6},{6,7},{7,0},{8,9},{9,10},{10,1... | collective-permute-start | bytes 3170312 | tf_op jit(solution)/shard_map/ppermute | solution.py:26
  38.0 21.7 %collective-permute-start.9 = (f32[1520,128]{1,0:T(8,128)S(1)}, f32[1520,128]{1,0:T(8,128)S(1)}, u32[]{:S(2)}, u32[]{:S(2)}) collective-permute-start(f32[1520,128]{1,0:T(8,128)S(1)} %pack.22), channel_id=1, source_target_pairs={{0,8},{1,9},{2,10},{3,11},{4,12},{5,13},{6,14},{7,15},{8,16},{9,17... | collective-permute-start | bytes 2334728 | tf_op jit(solution)/shard_map/ppermute | solution.py:26
  45.2 24.0 %collective-permute-start.10 = (f32[2272,128]{1,0:T(8,128)S(1)}, f32[2272,128]{1,0:T(8,128)S(1)}, u32[]{:S(2)}, u32[]{:S(2)}) collective-permute-start(f32[2272,128]{1,0:T(8,128)S(1)} %pack.23), channel_id=1, source_target_pairs={{0,7},{1,0},{2,1},{3,2},{4,3},{5,4},{6,5},{7,6},{8,15},{9,8},{10,9... | collective-permute-start | bytes 3489800 | tf_op jit(solution)/shard_map/ppermute | solution.py:26
  46.3 23.1 %collective-permute-start.11 = (f32[1824,128]{1,0:T(8,128)S(1)}, f32[1824,128]{1,0:T(8,128)S(1)}, u32[]{:S(2)}, u32[]{:S(2)}) collective-permute-start(f32[1824,128]{1,0:T(8,128)S(1)} %pack.24), channel_id=1, source_target_pairs={{0,24},{1,25},{2,26},{3,27},{4,28},{5,29},{6,30},{7,31},{8,0},{9,1... | collective-permute-start | bytes 2801672 | tf_op jit(solution)/shard_map/ppermute | solution.py:26
  58.7 18.4 %collective-permute-start.12 = (f32[1760,128]{1,0:T(8,128)S(1)}, f32[1760,128]{1,0:T(8,128)S(1)}, u32[]{:S(2)}, u32[]{:S(2)}) collective-permute-start(f32[1760,128]{1,0:T(8,128)S(1)} %pack.25), channel_id=1, source_target_pairs={{0,1},{1,2},{2,3},{3,4},{4,5},{5,6},{6,7},{7,0},{8,9},{9,10},{10,1... | collective-permute-start | bytes 2703368 | tf_op jit(solution)/shard_map/ppermute | solution.py:26
  59.8 17.4 %collective-permute-start.13 = (f32[1824,128]{1,0:T(8,128)S(1)}, f32[1824,128]{1,0:T(8,128)S(1)}, u32[]{:S(2)}, u32[]{:S(2)}) collective-permute-start(f32[1824,128]{1,0:T(8,128)S(1)} %pack.26), channel_id=1, source_target_pairs={{0,8},{1,9},{2,10},{3,11},{4,12},{5,13},{6,14},{7,15},{8,16},{9,17... | collective-permute-start | bytes 2801672 | tf_op jit(solution)/shard_map/ppermute | solution.py:26
  69.2 16.6 %collective-permute-start.14 = (f32[1760,128]{1,0:T(8,128)S(1)}, f32[1760,128]{1,0:T(8,128)S(1)}, u32[]{:S(2)}, u32[]{:S(2)}) collective-permute-start(f32[1760,128]{1,0:T(8,128)S(1)} %slice.9), channel_id=1, source_target_pairs={{0,7},{1,0},{2,1},{3,2},{4,3},{5,4},{6,5},{7,6},{8,15},{9,8},{10,9... | collective-permute-start | bytes 2703368 | tf_op jit(solution)/shard_map/ppermute | solution.py:26
  69.4 20.7 %collective-permute-start.15 = (f32[1824,128]{1,0:T(8,128)S(1)}, f32[1824,128]{1,0:T(8,128)S(1)}, u32[]{:S(2)}, u32[]{:S(2)}) collective-permute-start(f32[1824,128]{1,0:T(8,128)S(1)} %pack.27), channel_id=1, source_target_pairs={{0,24},{1,25},{2,26},{3,27},{4,28},{5,29},{6,30},{7,31},{8,0},{9,1... | collective-permute-start | bytes 2801672 | tf_op jit(solution)/shard_map/ppermute | solution.py:26
  77.2 18.3 %collective-permute-start.17 = (f32[1520,128]{1,0:T(8,128)S(1)}, f32[1520,128]{1,0:T(8,128)S(1)}, u32[]{:S(2)}, u32[]{:S(2)}) collective-permute-start(f32[1520,128]{1,0:T(8,128)S(1)} %pack.29), channel_id=1, source_target_pairs={{0,8},{1,9},{2,10},{3,11},{4,12},{5,13},{6,14},{7,15},{8,16},{9,17... | collective-permute-start | bytes 2334728 | tf_op jit(solution)/shard_map/ppermute | solution.py:26
  82.5 13.0 %collective-permute-start.16 = (f32[1040,128]{1,0:T(8,128)S(1)}, f32[1040,128]{1,0:T(8,128)S(1)}, u32[]{:S(2)}, u32[]{:S(2)}) collective-permute-start(f32[1040,128]{1,0:T(8,128)S(1)} %pack.28), channel_id=1, source_target_pairs={{0,1},{1,2},{2,3},{3,4},{4,5},{5,6},{6,7},{7,0},{8,9},{9,10},{10,1... | collective-permute-start | bytes 1597448 | tf_op jit(solution)/shard_map/ppermute | solution.py:26
  90.2 16.8 %collective-permute-start.19 = (f32[1216,128]{1,0:T(8,128)S(1)}, f32[1216,128]{1,0:T(8,128)S(1)}, u32[]{:S(2)}, u32[]{:S(2)}) collective-permute-start(f32[1216,128]{1,0:T(8,128)S(1)} %pack.31), channel_id=1, source_target_pairs={{0,24},{1,25},{2,26},{3,27},{4,28},{5,29},{6,30},{7,31},{8,0},{9,1... | collective-permute-start | bytes 1867784 | tf_op jit(solution)/shard_map/ppermute | solution.py:26
  90.3 12.7 %collective-permute-start.18 = (f32[832,128]{1,0:T(8,128)S(1)}, f32[832,128]{1,0:T(8,128)S(1)}, u32[]{:S(2)}, u32[]{:S(2)}) collective-permute-start(f32[832,128]{1,0:T(8,128)S(1)} %pack.30), channel_id=1, source_target_pairs={{0,7},{1,0},{2,1},{3,2},{4,3},{5,4},{6,5},{7,6},{8,15},{9,8},{10,9... | collective-permute-start | bytes 1277960 | tf_op jit(solution)/shard_map/ppermute | solution.py:26
  95.5 13.0 %collective-permute-start.21 = (f32[912,128]{1,0:T(8,128)S(1)}, f32[912,128]{1,0:T(8,128)S(1)}, u32[]{:S(2)}, u32[]{:S(2)}) collective-permute-start(f32[912,128]{1,0:T(8,128)S(1)} %pack.33), channel_id=1, source_target_pairs={{0,8},{1,9},{2,10},{3,11},{4,12},{5,13},{6,14},{7,15},{8,16},{9,17... | collective-permute-start | bytes 1400840 | tf_op jit(solution)/shard_map/ppermute | solution.py:26
  98.0 10.6 %collective-permute-start.20 = (f32[624,128]{1,0:T(8,128)S(1)}, f32[624,128]{1,0:T(8,128)S(1)}, u32[]{:S(2)}, u32[]{:S(2)}) collective-permute-start(f32[624,128]{1,0:T(8,128)S(1)} %pack.32), channel_id=1, source_target_pairs={{0,1},{1,2},{2,3},{3,4},{4,5},{5,6},{6,7},{7,0},{8,9},{9,10},{10,1... | collective-permute-start | bytes 958472 | tf_op jit(solution)/shard_map/ppermute | solution.py:26
  103.0 6.7 %collective-permute-start.22 = (f32[208,128]{1,0:T(8,128)S(1)}, f32[208,128]{1,0:T(8,128)S(1)}, u32[]{:S(2)}, u32[]{:S(2)}) collective-permute-start(f32[208,128]{1,0:T(8,128)S(1)} %slice.10), channel_id=1, source_target_pairs={{0,7},{1,0},{2,1},{3,2},{4,3},{5,4},{6,5},{7,6},{8,15},{9,8},{10,9... | collective-permute-start | bytes 319496 | tf_op jit(solution)/shard_map/ppermute | solution.py:26
  107.0 6.5 %collective-permute-start.23 = (f32[304,128]{1,0:T(8,128)S(1)}, f32[304,128]{1,0:T(8,128)S(1)}, u32[]{:S(2)}, u32[]{:S(2)}) collective-permute-start(f32[304,128]{1,0:T(8,128)S(1)} %slice.11), channel_id=1, source_target_pairs={{0,24},{1,25},{2,26},{3,27},{4,28},{5,29},{6,30},{7,31},{8,0},{9,1... | collective-permute-start | bytes 466952 | tf_op jit(solution)/shard_map/ppermute | solution.py:26
  (3 other events, 23.1 us)

commit v3 on v2

--- a/solution.py
+++ b/solution.py
@@ -17,13 +17,11 @@
 
 def shift(v, axis, d):
     pairs = []
-    for row in range(lax.axis_size("row")):
-        step = d if row % 2 == 0 else -d
-        for x in range(NX):
-            for z in range(NZ):
-                to = (x + step) % NX * NZ + z if axis == "x" else x * NZ + (z + step) % NZ
-                pairs.append((row * NX * NZ + x * NZ + z, row * NX * NZ + to))
-    return lax.ppermute(v, ("row", "col"), pairs)
+    for x in range(NX):
+        for z in range(NZ):
+            to = (x + d) % NX * NZ + z if axis == "x" else x * NZ + (z + d) % NZ
+            pairs.append((x * NZ + z, to))
+    return lax.ppermute(v, "col", pairs)
 
 
 def cost(flops):
@@ -293,9 +291,8 @@
     blocks = tuple((sum(heights[:i]), h) for i, h in enumerate(heights))
     me = lax.axis_index("col")
     x, z = me // NZ, me % NZ
-    way = 1 - 2 * (lax.axis_index("row") % 2)
-    xs = (x + way * jnp.array(XPOS)) % NX
-    zs = (z + way * jnp.array(ZPOS)) % NZ
+    xs = (x + jnp.array(XPOS)) % NX
+    zs = (z + jnp.array(ZPOS)) % NZ
     order = slab_order[(zs[:, None] + xs[None, :] * NZ).reshape(-1)]
 
     line = Line(jnp.zeros((8, T), jnp.float32))

time: 153 us -> 148 us (0.967)
  starting transfers between devices: 39.4 us -> 35 us
  blocking collectives: 34.6 us -> 32.6 us
    ppermute x24, starting transfers between devices: 39.4 us -> 35 us  [shift(): return lax.ppermute(v, 'col', pairs)]
    all_to_all x2, blocking collectives: 34.6 us -> 32.6 us  [local(): lax.all_to_all(jnp.broadcast_to(energy, (size, 8, T)), axis, 0, 0)]
  transfers between devices with their start and end apart: 24 -> 24, of which waited for: 12 -> 15; matrix products, arithmetic and copies ran while one was open for 2% -> 2% of each run, Pallas kernels for 15% -> 16%
where the time goes in v3:
time: 148 us; the launch traced here: 147 us
  waiting for transfers between devices  47.8 us (32%)
  starting transfers between devices  35 us (24%)
  blocking collectives  32.6 us (22%)
  Pallas kernels  25.4 us (17%)
  between operations  2.78 us (2%)
  other arithmetic  2.06 us (1%)
  local copies, waits for them, and re-layouts  1.66 us (1%)
    ppermute x24, waiting for transfers between devices, shift(): return lax.ppermute(v, 'col', pairs)  47.8 us
    ppermute x24, starting transfers between devices, shift(): return lax.ppermute(v, 'col', pairs)  35 us
    all_to_all x2, blocking collectives, local(): lax.all_to_all(jnp.broadcast_to(energy, (size, 8, T)), axis, 0, 0)  32.6 us
    pallas_call x11, Pallas kernels, middle(): pl.pallas_call(functools.partial(middle_kernel, blocks, work, n, not tota...  17.8 us
    pallas_call x1, Pallas kernels, prepare(): pl.pallas_call(prepare_kernel, out_shape=[pltpu.VMEM((depth, width), jnp....  4.59 us
  transfers between devices with their start and end apart: 24, of which 15 were waited for; matrix products, arithmetic and copies ran while one was open for 2% of the time, Pallas kernels for 16%

profile of v3, /device:TPU:1, one launch (start us, length us, event | category | flops | bytes accessed | tf_op | source)
XLA Modules:
  0.0 147.3 jit_solution(13068608054230746872)
XLA Ops:
  0.6 2.5 %collective-permute-start.1 = (f32[1024,128]{1,0:T(8,128)}, f32[1024,128]{1,0:T(8,128)S(1)}, u32[]{:S(2)}, u32[]{:S(2)}) collective-permute-start(f32[1024,128]{1,0:T(8,128)} %refs_0_.1), channel_id=1, source_target_pairs={{0,1},{1,2},{2,3},{3,4},{4,5},{5,6},{6,7},{7,0},{8,9},{9,10},{10,1... | collective-permute-start | bytes 1572872 | tf_op jit(solution)/shard_map/ppermute | solution.py:24
  8.1 4.0 %collective-permute-start.3 = (f32[1024,128]{1,0:T(8,128)}, f32[1024,128]{1,0:T(8,128)S(1)}, u32[]{:S(2)}, u32[]{:S(2)}) collective-permute-start(f32[1024,128]{1,0:T(8,128)} %refs_0_.1), channel_id=1, source_target_pairs={{0,7},{1,0},{2,1},{3,2},{4,3},{5,4},{6,5},{7,6},{8,15},{9,8},{10,9... | collective-permute-start | bytes 1572872 | tf_op jit(solution)/shard_map/ppermute | solution.py:24
  12.9 4.6 %prepare.1 = (bf16[4096,512]{1,0:T(8,128)(2,1)S(1)}, bf16[4096,512]{1,0:T(8,128)(2,1)S(1)}) custom-call(s32[32]{0:T(128)S(1)} %gather_fusion, s32[32,4]{1,0:T(8,128)S(1)} %copy.21.screen_ref, f32[4096,512]{1,0:T(8,128)} %b_ref), custom_call_target="tpu_custom_call" | custom-call | flops 1 | tf_op jit(solution)/shard_map/prepare/pallas_call | solution.py:119
  22.5 3.4 %collective-permute-start.7 = (f32[1856,128]{1,0:T(8,128)S(1)}, f32[1856,128]{1,0:T(8,128)S(1)}, u32[]{:S(2)}, u32[]{:S(2)}) collective-permute-start(f32[1856,128]{1,0:T(8,128)S(1)} %pack.19), channel_id=1, source_target_pairs={{0,7},{1,0},{2,1},{3,2},{4,3},{5,4},{6,5},{7,6},{8,15},{9,8},{10,9... | collective-permute-start | bytes 2850824 | tf_op jit(solution)/shard_map/ppermute | solution.py:24
  28.4 4.7 %collective-permute-done.4.refs_2_.refs_0_.refs_1_ = f32[1120,128]{1,0:T(8,128)S(1)} collective-permute-done((f32[1120,128]{1,0:T(8,128)S(1)}, f32[1120,128]{1,0:T(8,128)S(1)}, u32[]{:S(2)}, u32[]{:S(2)}) %collective-permute-start.4) | collective-permute-done | bytes 573472 | tf_op jit(solution)/shard_map/ppermute | solution.py:24
  33.1 4.0 %collective-permute-done.5.refs_0_.refs_1_ = f32[1440,128]{1,0:T(8,128)S(1)} collective-permute-done((f32[1440,128]{1,0:T(8,128)S(1)}, f32[1440,128]{1,0:T(8,128)S(1)}, u32[]{:S(2)}, u32[]{:S(2)}) %collective-permute-start.5) | collective-permute-done | bytes 737312 | tf_op jit(solution)/shard_map/ppermute | solution.py:24
  40.1 4.7 %collective-permute-done.6.refs_2_.refs_0_.refs_1_ = f32[1728,128]{1,0:T(8,128)S(1)} collective-permute-done((f32[1728,128]{1,0:T(8,128)S(1)}, f32[1728,128]{1,0:T(8,128)S(1)}, u32[]{:S(2)}, u32[]{:S(2)}) %collective-permute-start.6) | collective-permute-done | bytes 884768 | tf_op jit(solution)/shard_map/ppermute | solution.py:24
  44.8 2.8 %collective-permute-start.10 = (f32[2272,128]{1,0:T(8,128)S(1)}, f32[2272,128]{1,0:T(8,128)S(1)}, u32[]{:S(2)}, u32[]{:S(2)}) collective-permute-start(f32[2272,128]{1,0:T(8,128)S(1)} %pack.23), channel_id=1, source_target_pairs={{0,7},{1,0},{2,1},{3,2},{4,3},{5,4},{6,5},{7,6},{8,15},{9,8},{10,9... | collective-permute-start | bytes 3489800 | tf_op jit(solution)/shard_map/ppermute | solution.py:24
  51.1 10.0 %collective-permute-done.8.refs_0_.refs_1_ = f32[2064,128]{1,0:T(8,128)S(1)} collective-permute-done((f32[2064,128]{1,0:T(8,128)S(1)}, f32[2064,128]{1,0:T(8,128)S(1)}, u32[]{:S(2)}, u32[]{:S(2)}) %collective-permute-start.8) | collective-permute-done | bytes 1056800 | tf_op jit(solution)/shard_map/ppermute | solution.py:24
  62.7 1.9 %middle.15.refs_4_ = f32[1024,512]{1,0:T(8,128)S(1)} custom-call(f32[2064,128]{1,0:T(8,128)S(1)} %collective-permute-done.8.refs_0_.refs_1_, f32[1520,128]{1,0:T(8,128)S(1)} %collective-permute-done.9.refs_2_.refs_1_, bf16[4096,512]{1,0:T(8,128)(2,1)S(1)} %get-tuple-element.135.refs_3_.refs_2_, ...), custom_call_target="tpu_custom_call", output_to_operand_aliasing={{}: (4, {})} | custom-call | flops 1000000000 | tf_op jit(solution)/shard_map/middle/pallas_call | solution.py:161
  64.5 5.0 %collective-permute-done.10.refs_1_.refs_0_ = f32[2272,128]{1,0:T(8,128)S(1)} collective-permute-done((f32[2272,128]{1,0:T(8,128)S(1)}, f32[2272,128]{1,0:T(8,128)S(1)}, u32[]{:S(2)}, u32[]{:S(2)}) %collective-permute-start.10) | collective-permute-done | bytes 1163296 | tf_op jit(solution)/shard_map/ppermute | solution.py:24
  69.6 3.5 %collective-permute-start.14 = (f32[1760,128]{1,0:T(8,128)S(1)}, f32[1760,128]{1,0:T(8,128)S(1)}, u32[]{:S(2)}, u32[]{:S(2)}) collective-permute-start(f32[1760,128]{1,0:T(8,128)S(1)} %slice.9), channel_id=1, source_target_pairs={{0,7},{1,0},{2,1},{3,2},{4,3},{5,4},{6,5},{7,6},{8,15},{9,8},{10,9... | collective-permute-start | bytes 2703368 | tf_op jit(solution)/shard_map/ppermute | solution.py:24
  74.5 2.1 %middle.16.refs_4_ = f32[1024,512]{1,0:T(8,128)S(1)} custom-call(f32[2272,128]{1,0:T(8,128)S(1)} %collective-permute-done.10.refs_1_.refs_0_, f32[1824,128]{1,0:T(8,128)S(1)} %collective-permute-done.11.refs_2_.refs_1_, bf16[4096,512]{1,0:T(8,128)(2,1)S(1)} %get-tuple-element.135.refs_3_.refs_2_, ...), custom_call_target="tpu_custom_call", output_to_operand_aliasing={{}: (4, {})} | custom-call | flops 1000000000 | tf_op jit(solution)/shard_map/middle/pallas_call | solution.py:161
  76.6 4.3 %collective-permute-done.12.refs_0_.refs_1_ = f32[1760,128]{1,0:T(8,128)S(1)} collective-permute-done((f32[1760,128]{1,0:T(8,128)S(1)}, f32[1760,128]{1,0:T(8,128)S(1)}, u32[]{:S(2)}, u32[]{:S(2)}) %collective-permute-start.12) | collective-permute-done | bytes 901152 | tf_op jit(solution)/shard_map/ppermute | solution.py:24
  82.3 1.9 %middle.17.refs_4_ = f32[1024,512]{1,0:T(8,128)S(1)} custom-call(f32[1760,128]{1,0:T(8,128)S(1)} %collective-permute-done.12.refs_0_.refs_1_, f32[1824,128]{1,0:T(8,128)S(1)} %collective-permute-done.13.refs_2_.refs_1_, bf16[4096,512]{1,0:T(8,128)(2,1)S(1)} %get-tuple-element.135.refs_3_.refs_2_, ...), custom_call_target="tpu_custom_call", output_to_operand_aliasing={{}: (4, {})} | custom-call | flops 1000000000 | tf_op jit(solution)/shard_map/middle/pallas_call | solution.py:161
  84.2 4.2 %collective-permute-done.14.refs_0_.refs_1_ = f32[1760,128]{1,0:T(8,128)S(1)} collective-permute-done((f32[1760,128]{1,0:T(8,128)S(1)}, f32[1760,128]{1,0:T(8,128)S(1)}, u32[]{:S(2)}, u32[]{:S(2)}) %collective-permute-start.14) | collective-permute-done | bytes 901152 | tf_op jit(solution)/shard_map/ppermute | solution.py:24
  88.4 2.7 %collective-permute-done.15.refs_2_.refs_1_ = f32[1824,128]{1,0:T(8,128)S(1)} collective-permute-done((f32[1824,128]{1,0:T(8,128)S(1)}, f32[1824,128]{1,0:T(8,128)S(1)}, u32[]{:S(2)}, u32[]{:S(2)}) %collective-permute-start.15) | collective-permute-done | bytes 933920 | tf_op jit(solution)/shard_map/ppermute | solution.py:24
  91.2 2.6 %collective-permute-start.19 = (f32[1216,128]{1,0:T(8,128)S(1)}, f32[1216,128]{1,0:T(8,128)S(1)}, u32[]{:S(2)}, u32[]{:S(2)}) collective-permute-start(f32[1216,128]{1,0:T(8,128)S(1)} %pack.31), channel_id=1, source_target_pairs={{0,24},{1,25},{2,26},{3,27},{4,28},{5,29},{6,30},{7,31},{8,0},{9,1... | collective-permute-start | bytes 1867784 | tf_op jit(solution)/shard_map/ppermute | solution.py:24
  94.0 1.9 %middle.18.refs_4_ = f32[1024,512]{1,0:T(8,128)S(1)} custom-call(f32[1760,128]{1,0:T(8,128)S(1)} %collective-permute-done.14.refs_0_.refs_1_, f32[1824,128]{1,0:T(8,128)S(1)} %collective-permute-done.15.refs_2_.refs_1_, bf16[4096,512]{1,0:T(8,128)(2,1)S(1)} %get-tuple-element.135.refs_3_.refs_2_, ...), custom_call_target="tpu_custom_call", output_to_operand_aliasing={{}: (4, {})} | custom-call | flops 1000000000 | tf_op jit(solution)/shard_map/middle/pallas_call | solution.py:161
  95.9 2.1 %collective-permute-done.17.refs_1_ = f32[1520,128]{1,0:T(8,128)S(1)} collective-permute-done((f32[1520,128]{1,0:T(8,128)S(1)}, f32[1520,128]{1,0:T(8,128)S(1)}, u32[]{:S(2)}, u32[]{:S(2)}) %collective-permute-start.17) | collective-permute-done | bytes 778272 | tf_op jit(solution)/shard_map/ppermute | solution.py:24
  103.6 2.5 %collective-permute-start.23 = (f32[304,128]{1,0:T(8,128)S(1)}, f32[304,128]{1,0:T(8,128)S(1)}, u32[]{:S(2)}, u32[]{:S(2)}) collective-permute-start(f32[304,128]{1,0:T(8,128)S(1)} %slice.11), channel_id=1, source_target_pairs={{0,24},{1,25},{2,26},{3,27},{4,28},{5,29},{6,30},{7,31},{8,0},{9,1... | collective-permute-start | bytes 466952 | tf_op jit(solution)/shard_map/ppermute | solution.py:24
  110.1 2.2 %last.1 = (f32[1024,512]{1,0:T(8,128)}, f32[8,128]{1,0:T(8,128)S(1)}) custom-call(f32[208,128]{1,0:T(8,128)S(1)} %collective-permute-done.22.refs_0_, f32[304,128]{1,0:T(8,128)S(1)} %collective-permute-done.23.refs_1_, bf16[4096,512]{1,0:T(8,128)(2,1)S(1)} %get-tuple-element.135.refs_3_.refs_2_, bf16[4096,512]{1,0:T(8,128)(2,1)S(1)} %get-tuple-element.136.refs_4_.refs_3_, ...), custom_call_target="tpu_custom_call" | custom-call | tf_op jit(solution)/shard_map/last/pallas_call | solution.py:190
  112.3 16.0 %all_to_all.10 = f32[8,8,128]{2,1,0:T(8,128)S(1)} all-to-all(f32[8,8,128]{2,1,0:T(8,128)S(1)} %broadcast_in_dim.13), channel_id=1, replica_groups=mesh['row'=8,'col'=32] {'row'}, dimensions={0} | all-to-all | bytes 65536 | tf_op jit(solution)/shard_map/all_to_all | solution.py:347
  128.3 16.6 %all_to_all.11 = f32[32,8,128]{2,1,0:T(8,128)S(1)} all-to-all(f32[32,8,128]{2,1,0:T(8,128)S(1)} %broadcast_in_dim.14), channel_id=1, replica_groups=mesh['row'=8,'col'=32] {'col'}, dimensions={0} | all-to-all | bytes 262144 | tf_op jit(solution)/shard_map/all_to_all | solution.py:347
  (84 shorter events, 34.5 us)
Async XLA Ops:
  0.6 18.3 %collective-permute-start.1 = (f32[1024,128]{1,0:T(8,128)}, f32[1024,128]{1,0:T(8,128)S(1)}, u32[]{:S(2)}, u32[]{:S(2)}) collective-permute-start(f32[1024,128]{1,0:T(8,128)} %refs_0_.1), channel_id=1, source_target_pairs={{0,1},{1,2},{2,3},{3,4},{4,5},{5,6},{6,7},{7,0},{8,9},{9,10},{10,1... | collective-permute-start | bytes 1572872 | tf_op jit(solution)/shard_map/ppermute | solution.py:24
  3.2 14.4 %collective-permute-start = (f32[1024,128]{1,0:T(8,128)}, f32[1024,128]{1,0:T(8,128)S(1)}, u32[]{:S(2)}, u32[]{:S(2)}) collective-permute-start(f32[1024,128]{1,0:T(8,128)} %refs_0_.1), channel_id=1, source_target_pairs={{0,8},{1,9},{2,10},{3,11},{4,12},{5,13},{6,14},{7,15},{8,16},{9,17... | collective-permute-start | bytes 1572872 | tf_op jit(solution)/shard_map/ppermute | solution.py:24
  6.6 15.7 %collective-permute-start.2 = (f32[1024,128]{1,0:T(8,128)}, f32[1024,128]{1,0:T(8,128)S(1)}, u32[]{:S(2)}, u32[]{:S(2)}) collective-permute-start(f32[1024,128]{1,0:T(8,128)} %refs_0_.1), channel_id=1, source_target_pairs={{0,24},{1,25},{2,26},{3,27},{4,28},{5,29},{6,30},{7,31},{8,0},{9,1... | collective-permute-start | bytes 1572872 | tf_op jit(solution)/shard_map/ppermute | solution.py:24
  8.1 14.3 %collective-permute-start.3 = (f32[1024,128]{1,0:T(8,128)}, f32[1024,128]{1,0:T(8,128)S(1)}, u32[]{:S(2)}, u32[]{:S(2)}) collective-permute-start(f32[1024,128]{1,0:T(8,128)} %refs_0_.1), channel_id=1, source_target_pairs={{0,7},{1,0},{2,1},{3,2},{4,3},{5,4},{6,5},{7,6},{8,15},{9,8},{10,9... | collective-permute-start | bytes 1572872 | tf_op jit(solution)/shard_map/ppermute | solution.py:24
  19.0 18.0 %collective-permute-start.5 = (f32[1440,128]{1,0:T(8,128)S(1)}, f32[1440,128]{1,0:T(8,128)S(1)}, u32[]{:S(2)}, u32[]{:S(2)}) collective-permute-start(f32[1440,128]{1,0:T(8,128)S(1)} %pack.17), channel_id=1, source_target_pairs={{0,1},{1,2},{2,3},{3,4},{4,5},{5,6},{6,7},{7,0},{8,9},{9,10},{10,1... | collective-permute-start | bytes 2211848 | tf_op jit(solution)/shard_map/ppermute | solution.py:24
  19.2 13.9 %collective-permute-start.4 = (f32[1120,128]{1,0:T(8,128)S(1)}, f32[1120,128]{1,0:T(8,128)S(1)}, u32[]{:S(2)}, u32[]{:S(2)}) collective-permute-start(f32[1120,128]{1,0:T(8,128)S(1)} %pack.18), channel_id=1, source_target_pairs={{0,8},{1,9},{2,10},{3,11},{4,12},{5,13},{6,14},{7,15},{8,16},{9,17... | collective-permute-start | bytes 1720328 | tf_op jit(solution)/shard_map/ppermute | solution.py:24
  22.5 22.2 %collective-permute-start.7 = (f32[1856,128]{1,0:T(8,128)S(1)}, f32[1856,128]{1,0:T(8,128)S(1)}, u32[]{:S(2)}, u32[]{:S(2)}) collective-permute-start(f32[1856,128]{1,0:T(8,128)S(1)} %pack.19), channel_id=1, source_target_pairs={{0,7},{1,0},{2,1},{3,2},{4,3},{5,4},{6,5},{7,6},{8,15},{9,8},{10,9... | collective-permute-start | bytes 2850824 | tf_op jit(solution)/shard_map/ppermute | solution.py:24
  26.0 18.8 %collective-permute-start.6 = (f32[1728,128]{1,0:T(8,128)S(1)}, f32[1728,128]{1,0:T(8,128)S(1)}, u32[]{:S(2)}, u32[]{:S(2)}) collective-permute-start(f32[1728,128]{1,0:T(8,128)S(1)} %pack.20), channel_id=1, source_target_pairs={{0,24},{1,25},{2,26},{3,27},{4,28},{5,29},{6,30},{7,31},{8,0},{9,1... | collective-permute-start | bytes 2654216 | tf_op jit(solution)/shard_map/ppermute | solution.py:24
  37.2 24.0 %collective-permute-start.8 = (f32[2064,128]{1,0:T(8,128)S(1)}, f32[2064,128]{1,0:T(8,128)S(1)}, u32[]{:S(2)}, u32[]{:S(2)}) collective-permute-start(f32[2064,128]{1,0:T(8,128)S(1)} %pack.21), channel_id=1, source_target_pairs={{0,1},{1,2},{2,3},{3,4},{4,5},{5,6},{6,7},{7,0},{8,9},{9,10},{10,1... | collective-permute-start | bytes 3170312 | tf_op jit(solution)/shard_map/ppermute | solution.py:24
  37.3 24.0 %collective-permute-start.9 = (f32[1520,128]{1,0:T(8,128)S(1)}, f32[1520,128]{1,0:T(8,128)S(1)}, u32[]{:S(2)}, u32[]{:S(2)}) collective-permute-start(f32[1520,128]{1,0:T(8,128)S(1)} %pack.22), channel_id=1, source_target_pairs={{0,8},{1,9},{2,10},{3,11},{4,12},{5,13},{6,14},{7,15},{8,16},{9,17... | collective-permute-start | bytes 2334728 | tf_op jit(solution)/shard_map/ppermute | solution.py:24
  44.8 24.7 %collective-permute-start.10 = (f32[2272,128]{1,0:T(8,128)S(1)}, f32[2272,128]{1,0:T(8,128)S(1)}, u32[]{:S(2)}, u32[]{:S(2)}) collective-permute-start(f32[2272,128]{1,0:T(8,128)S(1)} %pack.23), channel_id=1, source_target_pairs={{0,7},{1,0},{2,1},{3,2},{4,3},{5,4},{6,5},{7,6},{8,15},{9,8},{10,9... | collective-permute-start | bytes 3489800 | tf_op jit(solution)/shard_map/ppermute | solution.py:24
  47.7 25.3 %collective-permute-start.11 = (f32[1824,128]{1,0:T(8,128)S(1)}, f32[1824,128]{1,0:T(8,128)S(1)}, u32[]{:S(2)}, u32[]{:S(2)}) collective-permute-start(f32[1824,128]{1,0:T(8,128)S(1)} %pack.24), channel_id=1, source_target_pairs={{0,24},{1,25},{2,26},{3,27},{4,28},{5,29},{6,30},{7,31},{8,0},{9,1... | collective-permute-start | bytes 2801672 | tf_op jit(solution)/shard_map/ppermute | solution.py:24
  61.2 19.7 %collective-permute-start.12 = (f32[1760,128]{1,0:T(8,128)S(1)}, f32[1760,128]{1,0:T(8,128)S(1)}, u32[]{:S(2)}, u32[]{:S(2)}) collective-permute-start(f32[1760,128]{1,0:T(8,128)S(1)} %pack.25), channel_id=1, source_target_pairs={{0,1},{1,2},{2,3},{3,4},{4,5},{5,6},{6,7},{7,0},{8,9},{9,10},{10,1... | collective-permute-start | bytes 2703368 | tf_op jit(solution)/shard_map/ppermute | solution.py:24
  61.4 20.4 %collective-permute-start.13 = (f32[1824,128]{1,0:T(8,128)S(1)}, f32[1824,128]{1,0:T(8,128)S(1)}, u32[]{:S(2)}, u32[]{:S(2)}) collective-permute-start(f32[1824,128]{1,0:T(8,128)S(1)} %pack.26), channel_id=1, source_target_pairs={{0,8},{1,9},{2,10},{3,11},{4,12},{5,13},{6,14},{7,15},{8,16},{9,17... | collective-permute-start | bytes 2801672 | tf_op jit(solution)/shard_map/ppermute | solution.py:24
  69.6 18.8 %collective-permute-start.14 = (f32[1760,128]{1,0:T(8,128)S(1)}, f32[1760,128]{1,0:T(8,128)S(1)}, u32[]{:S(2)}, u32[]{:S(2)}) collective-permute-start(f32[1760,128]{1,0:T(8,128)S(1)} %slice.9), channel_id=1, source_target_pairs={{0,7},{1,0},{2,1},{3,2},{4,3},{5,4},{6,5},{7,6},{8,15},{9,8},{10,9... | collective-permute-start | bytes 2703368 | tf_op jit(solution)/shard_map/ppermute | solution.py:24
  73.1 18.0 %collective-permute-start.15 = (f32[1824,128]{1,0:T(8,128)S(1)}, f32[1824,128]{1,0:T(8,128)S(1)}, u32[]{:S(2)}, u32[]{:S(2)}) collective-permute-start(f32[1824,128]{1,0:T(8,128)S(1)} %pack.27), channel_id=1, source_target_pairs={{0,24},{1,25},{2,26},{3,27},{4,28},{5,29},{6,30},{7,31},{8,0},{9,1... | collective-permute-start | bytes 2801672 | tf_op jit(solution)/shard_map/ppermute | solution.py:24
  81.8 16.2 %collective-permute-start.17 = (f32[1520,128]{1,0:T(8,128)S(1)}, f32[1520,128]{1,0:T(8,128)S(1)}, u32[]{:S(2)}, u32[]{:S(2)}) collective-permute-start(f32[1520,128]{1,0:T(8,128)S(1)} %pack.29), channel_id=1, source_target_pairs={{0,8},{1,9},{2,10},{3,11},{4,12},{5,13},{6,14},{7,15},{8,16},{9,17... | collective-permute-start | bytes 2334728 | tf_op jit(solution)/shard_map/ppermute | solution.py:24
  82.3 13.6 %collective-permute-start.16 = (f32[1040,128]{1,0:T(8,128)S(1)}, f32[1040,128]{1,0:T(8,128)S(1)}, u32[]{:S(2)}, u32[]{:S(2)}) collective-permute-start(f32[1040,128]{1,0:T(8,128)S(1)} %pack.28), channel_id=1, source_target_pairs={{0,1},{1,2},{2,3},{3,4},{4,5},{5,6},{6,7},{7,0},{8,9},{9,10},{10,1... | collective-permute-start | bytes 1597448 | tf_op jit(solution)/shard_map/ppermute | solution.py:24
  91.2 12.5 %collective-permute-start.19 = (f32[1216,128]{1,0:T(8,128)S(1)}, f32[1216,128]{1,0:T(8,128)S(1)}, u32[]{:S(2)}, u32[]{:S(2)}) collective-permute-start(f32[1216,128]{1,0:T(8,128)S(1)} %pack.31), channel_id=1, source_target_pairs={{0,24},{1,25},{2,26},{3,27},{4,28},{5,29},{6,30},{7,31},{8,0},{9,1... | collective-permute-start | bytes 1867784 | tf_op jit(solution)/shard_map/ppermute | solution.py:24
  93.7 7.3 %collective-permute-start.18 = (f32[832,128]{1,0:T(8,128)S(1)}, f32[832,128]{1,0:T(8,128)S(1)}, u32[]{:S(2)}, u32[]{:S(2)}) collective-permute-start(f32[832,128]{1,0:T(8,128)S(1)} %pack.30), channel_id=1, source_target_pairs={{0,7},{1,0},{2,1},{3,2},{4,3},{5,4},{6,5},{7,6},{8,15},{9,8},{10,9... | collective-permute-start | bytes 1277960 | tf_op jit(solution)/shard_map/ppermute | solution.py:24
  98.0 9.6 %collective-permute-start.21 = (f32[912,128]{1,0:T(8,128)S(1)}, f32[912,128]{1,0:T(8,128)S(1)}, u32[]{:S(2)}, u32[]{:S(2)}) collective-permute-start(f32[912,128]{1,0:T(8,128)S(1)} %pack.33), channel_id=1, source_target_pairs={{0,8},{1,9},{2,10},{3,11},{4,12},{5,13},{6,14},{7,15},{8,16},{9,17... | collective-permute-start | bytes 1400840 | tf_op jit(solution)/shard_map/ppermute | solution.py:24
  98.1 9.5 %collective-permute-start.20 = (f32[624,128]{1,0:T(8,128)S(1)}, f32[624,128]{1,0:T(8,128)S(1)}, u32[]{:S(2)}, u32[]{:S(2)}) collective-permute-start(f32[624,128]{1,0:T(8,128)S(1)} %pack.32), channel_id=1, source_target_pairs={{0,1},{1,2},{2,3},{3,4},{4,5},{5,6},{6,7},{7,0},{8,9},{9,10},{10,1... | collective-permute-start | bytes 958472 | tf_op jit(solution)/shard_map/ppermute | solution.py:24
  101.0 7.7 %collective-permute-start.22 = (f32[208,128]{1,0:T(8,128)S(1)}, f32[208,128]{1,0:T(8,128)S(1)}, u32[]{:S(2)}, u32[]{:S(2)}) collective-permute-start(f32[208,128]{1,0:T(8,128)S(1)} %slice.10), channel_id=1, source_target_pairs={{0,7},{1,0},{2,1},{3,2},{4,3},{5,4},{6,5},{7,6},{8,15},{9,8},{10,9... | collective-permute-start | bytes 319496 | tf_op jit(solution)/shard_map/ppermute | solution.py:24
  103.6 6.4 %collective-permute-start.23 = (f32[304,128]{1,0:T(8,128)S(1)}, f32[304,128]{1,0:T(8,128)S(1)}, u32[]{:S(2)}, u32[]{:S(2)}) collective-permute-start(f32[304,128]{1,0:T(8,128)S(1)} %slice.11), channel_id=1, source_target_pairs={{0,24},{1,25},{2,26},{3,27},{4,28},{5,29},{6,30},{7,31},{8,0},{9,1... | collective-permute-start | bytes 466952 | tf_op jit(solution)/shard_map/ppermute | solution.py:24
  (3 other events, 10.7 us)

commit v4 on v3

--- a/solution.py
+++ b/solution.py
@@ -285,7 +285,7 @@
 
 def local(amplitudes, integrals, screen, slab_order, weights):
     count = amplitudes.shape[0]
-    outer = count * 13 // 64
+    outer = count * 12 // 64
     inner = count // 2 - outer
     heights = (outer, inner, inner, outer)
     blocks = tuple((sum(heights[:i]), h) for i, h in enumerate(heights))
@@ -318,7 +318,7 @@
 
     for d in (1, -1):
         for axis in "xz":
-            send(axis, d, 0, () if d == 1 else (order,))
+            send(axis, d, 0)
     order, integrals = line.hold(order, integrals)
     high, low = line.hold(*prepare(order, screen, integrals))
     for k in range(1, len(SENDS["x", 1])):

time: 148 us -> 146 us (0.986)
  waiting for transfers between devices: 47.8 us -> 43.4 us
  starting transfers between devices: 35 us -> 38.3 us
    ppermute x24, waiting for transfers between devices: 47.8 us -> 43.4 us  [shift(): return lax.ppermute(v, 'col', pairs)]
    ppermute x24, starting transfers between devices: 35 us -> 38.3 us  [shift(): return lax.ppermute(v, 'col', pairs)]
  transfers between devices with their start and end apart: 24 -> 24, of which waited for: 15 -> 13; matrix products, arithmetic and copies ran while one was open for 2% -> 2% of each run, Pallas kernels for 16% -> 16%
where the time goes in v4:
time: 146 us
  waiting for transfers between devices  43.4 us (30%)
  starting transfers between devices  38.3 us (26%)
  blocking collectives  31.9 us (22%)
  Pallas kernels  25.5 us (17%)
  between operations  2.84 us (2%)
  other arithmetic  2.06 us (1%)
  local copies, waits for them, and re-layouts  1.67 us (1%)
    ppermute x24, waiting for transfers between devices, shift(): return lax.ppermute(v, 'col', pairs)  43.4 us
    ppermute x24, starting transfers between devices, shift(): return lax.ppermute(v, 'col', pairs)  38.3 us
    all_to_all x2, blocking collectives, local(): lax.all_to_all(jnp.broadcast_to(energy, (size, 8, T)), axis, 0, 0)  31.9 us
    pallas_call x11, Pallas kernels, middle(): pl.pallas_call(functools.partial(middle_kernel, blocks, work, n, not tota...  17.9 us
    pallas_call x1, Pallas kernels, prepare(): pl.pallas_call(prepare_kernel, out_shape=[pltpu.VMEM((depth, width), jnp....  4.59 us
  transfers between devices with their start and end apart: 24, of which 13 were waited for; matrix products, arithmetic and copies ran while one was open for 2% of the time, Pallas kernels for 16%

profile of v4, /device:TPU:1, one launch (start us, length us, event | category | flops | bytes accessed | tf_op | source)
XLA Modules:
  0.0 145.7 jit_solution(2429161522324442240)
XLA Ops:
  0.6 2.5 %collective-permute-start.1 = (f32[1024,128]{1,0:T(8,128)}, f32[1024,128]{1,0:T(8,128)S(1)}, u32[]{:S(2)}, u32[]{:S(2)}) collective-permute-start(f32[1024,128]{1,0:T(8,128)} %refs_0_.1), channel_id=1, source_target_pairs={{0,1},{1,2},{2,3},{3,4},{4,5},{5,6},{6,7},{7,0},{8,9},{9,10},{10,1... | collective-permute-start | bytes 1572872 | tf_op jit(solution)/shard_map/ppermute | solution.py:24
  4.4 4.0 %collective-permute-start.3 = (f32[1024,128]{1,0:T(8,128)}, f32[1024,128]{1,0:T(8,128)S(1)}, u32[]{:S(2)}, u32[]{:S(2)}) collective-permute-start(f32[1024,128]{1,0:T(8,128)} %refs_0_.1), channel_id=1, source_target_pairs={{0,7},{1,0},{2,1},{3,2},{4,3},{5,4},{6,5},{7,6},{8,15},{9,8},{10,9... | collective-permute-start | bytes 1572872 | tf_op jit(solution)/shard_map/ppermute | solution.py:24
  12.9 4.6 %prepare.1 = (bf16[4096,512]{1,0:T(8,128)(2,1)S(1)}, bf16[4096,512]{1,0:T(8,128)(2,1)S(1)}) custom-call(s32[32]{0:T(128)S(1)} %gather_fusion, s32[32,4]{1,0:T(8,128)S(1)} %copy.21.screen_ref, f32[4096,512]{1,0:T(8,128)} %b_ref), custom_call_target="tpu_custom_call" | custom-call | flops 1 | tf_op jit(solution)/shard_map/prepare/pallas_call | solution.py:119
  24.0 2.7 %collective-permute-start.7 = (f32[1792,128]{1,0:T(8,128)S(1)}, f32[1792,128]{1,0:T(8,128)S(1)}, u32[]{:S(2)}, u32[]{:S(2)}) collective-permute-start(f32[1792,128]{1,0:T(8,128)S(1)} %pack.19), channel_id=1, source_target_pairs={{0,7},{1,0},{2,1},{3,2},{4,3},{5,4},{6,5},{7,6},{8,15},{9,8},{10,9... | collective-permute-start | bytes 2752520 | tf_op jit(solution)/shard_map/ppermute | solution.py:24
  27.7 5.7 %collective-permute-done.4.refs_2_.refs_0_.refs_1_ = f32[1152,128]{1,0:T(8,128)S(1)} collective-permute-done((f32[1152,128]{1,0:T(8,128)S(1)}, f32[1152,128]{1,0:T(8,128)S(1)}, u32[]{:S(2)}, u32[]{:S(2)}) %collective-permute-start.4) | collective-permute-done | bytes 589856 | tf_op jit(solution)/shard_map/ppermute | solution.py:24
  33.4 3.3 %collective-permute-done.5.refs_0_.refs_1_ = f32[1408,128]{1,0:T(8,128)S(1)} collective-permute-done((f32[1408,128]{1,0:T(8,128)S(1)}, f32[1408,128]{1,0:T(8,128)S(1)}, u32[]{:S(2)}, u32[]{:S(2)}) %collective-permute-start.5) | collective-permute-done | bytes 720928 | tf_op jit(solution)/shard_map/ppermute | solution.py:24
  39.7 3.2 %collective-permute-done.6.refs_2_.refs_0_.refs_1_ = f32[1792,128]{1,0:T(8,128)S(1)} collective-permute-done((f32[1792,128]{1,0:T(8,128)S(1)}, f32[1792,128]{1,0:T(8,128)S(1)}, u32[]{:S(2)}, u32[]{:S(2)}) %collective-permute-start.6) | collective-permute-done | bytes 917536 | tf_op jit(solution)/shard_map/ppermute | solution.py:24
  44.3 3.5 %collective-permute-start.10 = (f32[2176,128]{1,0:T(8,128)S(1)}, f32[2176,128]{1,0:T(8,128)S(1)}, u32[]{:S(2)}, u32[]{:S(2)}) collective-permute-start(f32[2176,128]{1,0:T(8,128)S(1)} %pack.23), channel_id=1, source_target_pairs={{0,7},{1,0},{2,1},{3,2},{4,3},{5,4},{6,5},{7,6},{8,15},{9,8},{10,9... | collective-permute-start | bytes 3342344 | tf_op jit(solution)/shard_map/ppermute | solution.py:24
  51.2 8.6 %collective-permute-done.8.refs_0_.refs_1_ = f32[1984,128]{1,0:T(8,128)S(1)} collective-permute-done((f32[1984,128]{1,0:T(8,128)S(1)}, f32[1984,128]{1,0:T(8,128)S(1)}, u32[]{:S(2)}, u32[]{:S(2)}) %collective-permute-start.8) | collective-permute-done | bytes 1015840 | tf_op jit(solution)/shard_map/ppermute | solution.py:24
  63.2 5.4 %collective-permute-done.10.refs_1_.refs_0_ = f32[2176,128]{1,0:T(8,128)S(1)} collective-permute-done((f32[2176,128]{1,0:T(8,128)S(1)}, f32[2176,128]{1,0:T(8,128)S(1)}, u32[]{:S(2)}, u32[]{:S(2)}) %collective-permute-start.10) | collective-permute-done | bytes 1114144 | tf_op jit(solution)/shard_map/ppermute | solution.py:24
  68.8 1.9 %collective-permute-start.15 = (f32[1920,128]{1,0:T(8,128)S(1)}, f32[1920,128]{1,0:T(8,128)S(1)}, u32[]{:S(2)}, u32[]{:S(2)}) collective-permute-start(f32[1920,128]{1,0:T(8,128)S(1)} %pack.27), channel_id=1, source_target_pairs={{0,24},{1,25},{2,26},{3,27},{4,28},{5,29},{6,30},{7,31},{8,0},{9,1... | collective-permute-start | bytes 2949128 | tf_op jit(solution)/shard_map/ppermute | solution.py:24
  70.7 2.8 %collective-permute-start.14 = (f32[1664,128]{1,0:T(8,128)S(1)}, f32[1664,128]{1,0:T(8,128)S(1)}, u32[]{:S(2)}, u32[]{:S(2)}) collective-permute-start(f32[1664,128]{1,0:T(8,128)S(1)} %slice.9), channel_id=1, source_target_pairs={{0,7},{1,0},{2,1},{3,2},{4,3},{5,4},{6,5},{7,6},{8,15},{9,8},{10,9... | collective-permute-start | bytes 2555912 | tf_op jit(solution)/shard_map/ppermute | solution.py:24
  73.5 2.1 %middle.16.refs_4_ = f32[1024,512]{1,0:T(8,128)S(1)} custom-call(f32[2176,128]{1,0:T(8,128)S(1)} %collective-permute-done.10.refs_1_.refs_0_, f32[1920,128]{1,0:T(8,128)S(1)} %collective-permute-done.11.refs_2_.refs_1_, bf16[4096,512]{1,0:T(8,128)(2,1)S(1)} %get-tuple-element.134.refs_3_.refs_2_, ...), custom_call_target="tpu_custom_call", output_to_operand_aliasing={{}: (4, {})} | custom-call | flops 1000000000 | tf_op jit(solution)/shard_map/middle/pallas_call | solution.py:161
  75.7 4.0 %collective-permute-done.12.refs_0_.refs_1_ = f32[1664,128]{1,0:T(8,128)S(1)} collective-permute-done((f32[1664,128]{1,0:T(8,128)S(1)}, f32[1664,128]{1,0:T(8,128)S(1)}, u32[]{:S(2)}, u32[]{:S(2)}) %collective-permute-start.12) | collective-permute-done | bytes 852000 | tf_op jit(solution)/shard_map/ppermute | solution.py:24
  81.8 1.9 %middle.17.refs_4_ = f32[1024,512]{1,0:T(8,128)S(1)} custom-call(f32[1664,128]{1,0:T(8,128)S(1)} %collective-permute-done.12.refs_0_.refs_1_, f32[1920,128]{1,0:T(8,128)S(1)} %collective-permute-done.13.refs_2_.refs_1_, bf16[4096,512]{1,0:T(8,128)(2,1)S(1)} %get-tuple-element.134.refs_3_.refs_2_, ...), custom_call_target="tpu_custom_call", output_to_operand_aliasing={{}: (4, {})} | custom-call | flops 1000000000 | tf_op jit(solution)/shard_map/middle/pallas_call | solution.py:161
  83.7 3.9 %collective-permute-done.14.refs_0_.refs_1_ = f32[1664,128]{1,0:T(8,128)S(1)} collective-permute-done((f32[1664,128]{1,0:T(8,128)S(1)}, f32[1664,128]{1,0:T(8,128)S(1)}, u32[]{:S(2)}, u32[]{:S(2)}) %collective-permute-start.14) | collective-permute-done | bytes 852000 | tf_op jit(solution)/shard_map/ppermute | solution.py:24
  88.8 2.2 %collective-permute-start.19 = (f32[1280,128]{1,0:T(8,128)S(1)}, f32[1280,128]{1,0:T(8,128)S(1)}, u32[]{:S(2)}, u32[]{:S(2)}) collective-permute-start(f32[1280,128]{1,0:T(8,128)S(1)} %pack.31), channel_id=1, source_target_pairs={{0,24},{1,25},{2,26},{3,27},{4,28},{5,29},{6,30},{7,31},{8,0},{9,1... | collective-permute-start | bytes 1966088 | tf_op jit(solution)/shard_map/ppermute | solution.py:24
  91.1 3.1 %collective-permute-start.18 = (f32[768,128]{1,0:T(8,128)S(1)}, f32[768,128]{1,0:T(8,128)S(1)}, u32[]{:S(2)}, u32[]{:S(2)}) collective-permute-start(f32[768,128]{1,0:T(8,128)S(1)} %pack.30), channel_id=1, source_target_pairs={{0,7},{1,0},{2,1},{3,2},{4,3},{5,4},{6,5},{7,6},{8,15},{9,8},{10,9... | collective-permute-start | bytes 1179656 | tf_op jit(solution)/shard_map/ppermute | solution.py:24
  96.1 2.5 %collective-permute-done.17.refs_1_ = f32[1600,128]{1,0:T(8,128)S(1)} collective-permute-done((f32[1600,128]{1,0:T(8,128)S(1)}, f32[1600,128]{1,0:T(8,128)S(1)}, u32[]{:S(2)}, u32[]{:S(2)}) %collective-permute-start.17) | collective-permute-done | bytes 819232 | tf_op jit(solution)/shard_map/ppermute | solution.py:24
  100.3 2.7 %collective-permute-start.22 = (f32[192,128]{1,0:T(8,128)S(1)}, f32[192,128]{1,0:T(8,128)S(1)}, u32[]{:S(2)}, u32[]{:S(2)}) collective-permute-start(f32[192,128]{1,0:T(8,128)S(1)} %slice.10), channel_id=1, source_target_pairs={{0,7},{1,0},{2,1},{3,2},{4,3},{5,4},{6,5},{7,6},{8,15},{9,8},{10,9... | collective-permute-start | bytes 294920 | tf_op jit(solution)/shard_map/ppermute | solution.py:24
  103.1 2.7 %collective-permute-start.23 = (f32[320,128]{1,0:T(8,128)S(1)}, f32[320,128]{1,0:T(8,128)S(1)}, u32[]{:S(2)}, u32[]{:S(2)}) collective-permute-start(f32[320,128]{1,0:T(8,128)S(1)} %slice.11), channel_id=1, source_target_pairs={{0,24},{1,25},{2,26},{3,27},{4,28},{5,29},{6,30},{7,31},{8,0},{9,1... | collective-permute-start | bytes 491528 | tf_op jit(solution)/shard_map/ppermute | solution.py:24
  109.2 2.2 %last.1 = (f32[1024,512]{1,0:T(8,128)}, f32[8,128]{1,0:T(8,128)S(1)}) custom-call(f32[192,128]{1,0:T(8,128)S(1)} %collective-permute-done.22.refs_0_, f32[320,128]{1,0:T(8,128)S(1)} %collective-permute-done.23.refs_1_, bf16[4096,512]{1,0:T(8,128)(2,1)S(1)} %get-tuple-element.134.refs_3_.refs_2_, bf16[4096,512]{1,0:T(8,128)(2,1)S(1)} %get-tuple-element.135.refs_4_.refs_3_, ...), custom_call_target="tpu_custom_call" | custom-call | tf_op jit(solution)/shard_map/last/pallas_call | solution.py:190
  111.4 15.3 %all_to_all.10 = f32[8,8,128]{2,1,0:T(8,128)S(1)} all-to-all(f32[8,8,128]{2,1,0:T(8,128)S(1)} %broadcast_in_dim.13), channel_id=1, replica_groups=mesh['row'=8,'col'=32] {'row'}, dimensions={0} | all-to-all | bytes 65536 | tf_op jit(solution)/shard_map/all_to_all | solution.py:347
  126.7 16.6 %all_to_all.11 = f32[32,8,128]{2,1,0:T(8,128)S(1)} all-to-all(f32[32,8,128]{2,1,0:T(8,128)S(1)} %broadcast_in_dim.14), channel_id=1, replica_groups=mesh['row'=8,'col'=32] {'col'}, dimensions={0} | all-to-all | bytes 262144 | tf_op jit(solution)/shard_map/all_to_all | solution.py:347
  (84 shorter events, 35.4 us)
Async XLA Ops:
  0.6 18.3 %collective-permute-start.1 = (f32[1024,128]{1,0:T(8,128)}, f32[1024,128]{1,0:T(8,128)S(1)}, u32[]{:S(2)}, u32[]{:S(2)}) collective-permute-start(f32[1024,128]{1,0:T(8,128)} %refs_0_.1), channel_id=1, source_target_pairs={{0,1},{1,2},{2,3},{3,4},{4,5},{5,6},{6,7},{7,0},{8,9},{9,10},{10,1... | collective-permute-start | bytes 1572872 | tf_op jit(solution)/shard_map/ppermute | solution.py:24
  3.2 14.3 %collective-permute-start = (f32[1024,128]{1,0:T(8,128)}, f32[1024,128]{1,0:T(8,128)S(1)}, u32[]{:S(2)}, u32[]{:S(2)}) collective-permute-start(f32[1024,128]{1,0:T(8,128)} %refs_0_.1), channel_id=1, source_target_pairs={{0,8},{1,9},{2,10},{3,11},{4,12},{5,13},{6,14},{7,15},{8,16},{9,17... | collective-permute-start | bytes 1572872 | tf_op jit(solution)/shard_map/ppermute | solution.py:24
  4.4 17.9 %collective-permute-start.3 = (f32[1024,128]{1,0:T(8,128)}, f32[1024,128]{1,0:T(8,128)S(1)}, u32[]{:S(2)}, u32[]{:S(2)}) collective-permute-start(f32[1024,128]{1,0:T(8,128)} %refs_0_.1), channel_id=1, source_target_pairs={{0,7},{1,0},{2,1},{3,2},{4,3},{5,4},{6,5},{7,6},{8,15},{9,8},{10,9... | collective-permute-start | bytes 1572872 | tf_op jit(solution)/shard_map/ppermute | solution.py:24
  8.4 13.8 %collective-permute-start.2 = (f32[1024,128]{1,0:T(8,128)}, f32[1024,128]{1,0:T(8,128)S(1)}, u32[]{:S(2)}, u32[]{:S(2)}) collective-permute-start(f32[1024,128]{1,0:T(8,128)} %refs_0_.1), channel_id=1, source_target_pairs={{0,24},{1,25},{2,26},{3,27},{4,28},{5,29},{6,30},{7,31},{8,0},{9,1... | collective-permute-start | bytes 1572872 | tf_op jit(solution)/shard_map/ppermute | solution.py:24
  19.0 17.7 %collective-permute-start.5 = (f32[1408,128]{1,0:T(8,128)S(1)}, f32[1408,128]{1,0:T(8,128)S(1)}, u32[]{:S(2)}, u32[]{:S(2)}) collective-permute-start(f32[1408,128]{1,0:T(8,128)S(1)} %pack.17), channel_id=1, source_target_pairs={{0,1},{1,2},{2,3},{3,4},{4,5},{5,6},{6,7},{7,0},{8,9},{9,10},{10,1... | collective-permute-start | bytes 2162696 | tf_op jit(solution)/shard_map/ppermute | solution.py:24
  19.2 14.2 %collective-permute-start.4 = (f32[1152,128]{1,0:T(8,128)S(1)}, f32[1152,128]{1,0:T(8,128)S(1)}, u32[]{:S(2)}, u32[]{:S(2)}) collective-permute-start(f32[1152,128]{1,0:T(8,128)S(1)} %pack.18), channel_id=1, source_target_pairs={{0,8},{1,9},{2,10},{3,11},{4,12},{5,13},{6,14},{7,15},{8,16},{9,17... | collective-permute-start | bytes 1769480 | tf_op jit(solution)/shard_map/ppermute | solution.py:24
  22.4 20.4 %collective-permute-start.6 = (f32[1792,128]{1,0:T(8,128)S(1)}, f32[1792,128]{1,0:T(8,128)S(1)}, u32[]{:S(2)}, u32[]{:S(2)}) collective-permute-start(f32[1792,128]{1,0:T(8,128)S(1)} %pack.20), channel_id=1, source_target_pairs={{0,24},{1,25},{2,26},{3,27},{4,28},{5,29},{6,30},{7,31},{8,0},{9,1... | collective-permute-start | bytes 2752520 | tf_op jit(solution)/shard_map/ppermute | solution.py:24
  24.0 20.2 %collective-permute-start.7 = (f32[1792,128]{1,0:T(8,128)S(1)}, f32[1792,128]{1,0:T(8,128)S(1)}, u32[]{:S(2)}, u32[]{:S(2)}) collective-permute-start(f32[1792,128]{1,0:T(8,128)S(1)} %pack.19), channel_id=1, source_target_pairs={{0,7},{1,0},{2,1},{3,2},{4,3},{5,4},{6,5},{7,6},{8,15},{9,8},{10,9... | collective-permute-start | bytes 2752520 | tf_op jit(solution)/shard_map/ppermute | solution.py:24
  36.8 23.1 %collective-permute-start.8 = (f32[1984,128]{1,0:T(8,128)S(1)}, f32[1984,128]{1,0:T(8,128)S(1)}, u32[]{:S(2)}, u32[]{:S(2)}) collective-permute-start(f32[1984,128]{1,0:T(8,128)S(1)} %pack.21), channel_id=1, source_target_pairs={{0,1},{1,2},{2,3},{3,4},{4,5},{5,6},{6,7},{7,0},{8,9},{9,10},{10,1... | collective-permute-start | bytes 3047432 | tf_op jit(solution)/shard_map/ppermute | solution.py:24
  37.0 23.0 %collective-permute-start.9 = (f32[1600,128]{1,0:T(8,128)S(1)}, f32[1600,128]{1,0:T(8,128)S(1)}, u32[]{:S(2)}, u32[]{:S(2)}) collective-permute-start(f32[1600,128]{1,0:T(8,128)S(1)} %pack.22), channel_id=1, source_target_pairs={{0,8},{1,9},{2,10},{3,11},{4,12},{5,13},{6,14},{7,15},{8,16},{9,17... | collective-permute-start | bytes 2457608 | tf_op jit(solution)/shard_map/ppermute | solution.py:24
  44.3 24.4 %collective-permute-start.10 = (f32[2176,128]{1,0:T(8,128)S(1)}, f32[2176,128]{1,0:T(8,128)S(1)}, u32[]{:S(2)}, u32[]{:S(2)}) collective-permute-start(f32[2176,128]{1,0:T(8,128)S(1)} %pack.23), channel_id=1, source_target_pairs={{0,7},{1,0},{2,1},{3,2},{4,3},{5,4},{6,5},{7,6},{8,15},{9,8},{10,9... | collective-permute-start | bytes 3342344 | tf_op jit(solution)/shard_map/ppermute | solution.py:24
  47.8 20.9 %collective-permute-start.11 = (f32[1920,128]{1,0:T(8,128)S(1)}, f32[1920,128]{1,0:T(8,128)S(1)}, u32[]{:S(2)}, u32[]{:S(2)}) collective-permute-start(f32[1920,128]{1,0:T(8,128)S(1)} %pack.24), channel_id=1, source_target_pairs={{0,24},{1,25},{2,26},{3,27},{4,28},{5,29},{6,30},{7,31},{8,0},{9,1... | collective-permute-start | bytes 2949128 | tf_op jit(solution)/shard_map/ppermute | solution.py:24
  60.1 21.5 %collective-permute-start.13 = (f32[1920,128]{1,0:T(8,128)S(1)}, f32[1920,128]{1,0:T(8,128)S(1)}, u32[]{:S(2)}, u32[]{:S(2)}) collective-permute-start(f32[1920,128]{1,0:T(8,128)S(1)} %pack.26), channel_id=1, source_target_pairs={{0,8},{1,9},{2,10},{3,11},{4,12},{5,13},{6,14},{7,15},{8,16},{9,17... | collective-permute-start | bytes 2949128 | tf_op jit(solution)/shard_map/ppermute | solution.py:24
  61.3 18.3 %collective-permute-start.12 = (f32[1664,128]{1,0:T(8,128)S(1)}, f32[1664,128]{1,0:T(8,128)S(1)}, u32[]{:S(2)}, u32[]{:S(2)}) collective-permute-start(f32[1664,128]{1,0:T(8,128)S(1)} %pack.25), channel_id=1, source_target_pairs={{0,1},{1,2},{2,3},{3,4},{4,5},{5,6},{6,7},{7,0},{8,9},{9,10},{10,1... | collective-permute-start | bytes 2555912 | tf_op jit(solution)/shard_map/ppermute | solution.py:24
  68.8 20.0 %collective-permute-start.15 = (f32[1920,128]{1,0:T(8,128)S(1)}, f32[1920,128]{1,0:T(8,128)S(1)}, u32[]{:S(2)}, u32[]{:S(2)}) collective-permute-start(f32[1920,128]{1,0:T(8,128)S(1)} %pack.27), channel_id=1, source_target_pairs={{0,24},{1,25},{2,26},{3,27},{4,28},{5,29},{6,30},{7,31},{8,0},{9,1... | collective-permute-start | bytes 2949128 | tf_op jit(solution)/shard_map/ppermute | solution.py:24
  70.7 16.9 %collective-permute-start.14 = (f32[1664,128]{1,0:T(8,128)S(1)}, f32[1664,128]{1,0:T(8,128)S(1)}, u32[]{:S(2)}, u32[]{:S(2)}) collective-permute-start(f32[1664,128]{1,0:T(8,128)S(1)} %slice.9), channel_id=1, source_target_pairs={{0,7},{1,0},{2,1},{3,2},{4,3},{5,4},{6,5},{7,6},{8,15},{9,8},{10,9... | collective-permute-start | bytes 2555912 | tf_op jit(solution)/shard_map/ppermute | solution.py:24
  81.6 17.0 %collective-permute-start.17 = (f32[1600,128]{1,0:T(8,128)S(1)}, f32[1600,128]{1,0:T(8,128)S(1)}, u32[]{:S(2)}, u32[]{:S(2)}) collective-permute-start(f32[1600,128]{1,0:T(8,128)S(1)} %pack.29), channel_id=1, source_target_pairs={{0,8},{1,9},{2,10},{3,11},{4,12},{5,13},{6,14},{7,15},{8,16},{9,17... | collective-permute-start | bytes 2457608 | tf_op jit(solution)/shard_map/ppermute | solution.py:24
  81.7 14.4 %collective-permute-start.16 = (f32[960,128]{1,0:T(8,128)S(1)}, f32[960,128]{1,0:T(8,128)S(1)}, u32[]{:S(2)}, u32[]{:S(2)}) collective-permute-start(f32[960,128]{1,0:T(8,128)S(1)} %pack.28), channel_id=1, source_target_pairs={{0,1},{1,2},{2,3},{3,4},{4,5},{5,6},{6,7},{7,0},{8,9},{9,10},{10,1... | collective-permute-start | bytes 1474568 | tf_op jit(solution)/shard_map/ppermute | solution.py:24
  88.8 14.2 %collective-permute-start.19 = (f32[1280,128]{1,0:T(8,128)S(1)}, f32[1280,128]{1,0:T(8,128)S(1)}, u32[]{:S(2)}, u32[]{:S(2)}) collective-permute-start(f32[1280,128]{1,0:T(8,128)S(1)} %pack.31), channel_id=1, source_target_pairs={{0,24},{1,25},{2,26},{3,27},{4,28},{5,29},{6,30},{7,31},{8,0},{9,1... | collective-permute-start | bytes 1966088 | tf_op jit(solution)/shard_map/ppermute | solution.py:24
  91.1 9.2 %collective-permute-start.18 = (f32[768,128]{1,0:T(8,128)S(1)}, f32[768,128]{1,0:T(8,128)S(1)}, u32[]{:S(2)}, u32[]{:S(2)}) collective-permute-start(f32[768,128]{1,0:T(8,128)S(1)} %pack.30), channel_id=1, source_target_pairs={{0,7},{1,0},{2,1},{3,2},{4,3},{5,4},{6,5},{7,6},{8,15},{9,8},{10,9... | collective-permute-start | bytes 1179656 | tf_op jit(solution)/shard_map/ppermute | solution.py:24
  98.6 9.5 %collective-permute-start.21 = (f32[960,128]{1,0:T(8,128)S(1)}, f32[960,128]{1,0:T(8,128)S(1)}, u32[]{:S(2)}, u32[]{:S(2)}) collective-permute-start(f32[960,128]{1,0:T(8,128)S(1)} %pack.33), channel_id=1, source_target_pairs={{0,8},{1,9},{2,10},{3,11},{4,12},{5,13},{6,14},{7,15},{8,16},{9,17... | collective-permute-start | bytes 1474568 | tf_op jit(solution)/shard_map/ppermute | solution.py:24
  98.7 8.5 %collective-permute-start.20 = (f32[576,128]{1,0:T(8,128)S(1)}, f32[576,128]{1,0:T(8,128)S(1)}, u32[]{:S(2)}, u32[]{:S(2)}) collective-permute-start(f32[576,128]{1,0:T(8,128)S(1)} %pack.32), channel_id=1, source_target_pairs={{0,1},{1,2},{2,3},{3,4},{4,5},{5,6},{6,7},{7,0},{8,9},{9,10},{10,1... | collective-permute-start | bytes 884744 | tf_op jit(solution)/shard_map/ppermute | solution.py:24
  100.3 8.8 %collective-permute-start.22 = (f32[192,128]{1,0:T(8,128)S(1)}, f32[192,128]{1,0:T(8,128)S(1)}, u32[]{:S(2)}, u32[]{:S(2)}) collective-permute-start(f32[192,128]{1,0:T(8,128)S(1)} %slice.10), channel_id=1, source_target_pairs={{0,7},{1,0},{2,1},{3,2},{4,3},{5,4},{6,5},{7,6},{8,15},{9,8},{10,9... | collective-permute-start | bytes 294920 | tf_op jit(solution)/shard_map/ppermute | solution.py:24
  103.1 6.1 %collective-permute-start.23 = (f32[320,128]{1,0:T(8,128)S(1)}, f32[320,128]{1,0:T(8,128)S(1)}, u32[]{:S(2)}, u32[]{:S(2)}) collective-permute-start(f32[320,128]{1,0:T(8,128)S(1)} %slice.11), channel_id=1, source_target_pairs={{0,24},{1,25},{2,26},{3,27},{4,28},{5,29},{6,30},{7,31},{8,0},{9,1... | collective-permute-start | bytes 491528 | tf_op jit(solution)/shard_map/ppermute | solution.py:24
  (3 other events, 15.8 us)
